TPU v7x, 128 devices: a whole 4x4x4 slice. The times are simulated.
128 devices in a mesh: span: 16 (over y, z), normal: 8 (over x, core).
Axes of the slice: x: 4, y: 4, z: 4, core: 2. Of those that a mesh axis runs over, the one named last changes fastest.
Arguments:
- volume_fraction: float32 [256, 128, 1024], P('span', 'normal'), may hold values from 0.5 to 1.5
- droplet_momentum: float32 [3, 256, 128, 1024], P(None, 'span', 'normal'), may hold values from -0.5 to 0.5
- air_velocity: float32 [3, 256, 128, 1024], P(None, 'span', 'normal'), may hold values from -1 to 1
- drag: float32 [256, 128, 1024], P('span', 'normal'), may hold values from 0.5 to 3
- wall_owner: int32 [256, 1024, 1], P('span'), may hold values from 0 to 127; in each aligned block of 2048 rows (0 to 2047, 2048 to 4095, ..., all dimensions but the last counted through in order) at most 32 rows name the same one
- wall_face: int32 [256, 1024], P('span'), may hold values from 0 to 1023
- film: float32 [131072], P(('span', 'normal')), may hold values from 0.1 to 1
- ice: float32 [131072], P(('span', 'normal')), may hold values from 0 to 1
- cooling: float32 [131072], P(('span', 'normal')), may hold values from 0.2 to 2
- shed: float32 [131072], P(('span', 'normal')), may hold values from 0.2 to 0.8
- share: float32 [4, 131072], P(None, ('span', 'normal')), may hold values from 0.05 to 0.25
- upstream: int32 [4, 131072], P(None, ('span', 'normal')), may hold values from -1 to 131070, as said below
Outputs:
- fraction_out: float32 [256, 128, 1024], P('span', 'normal')
- momentum_out: float32 [3, 256, 128, 1024], P(None, 'span', 'normal')
- film_out: float32 [131072], P(('span', 'normal'))
- ice_out: float32 [131072], P(('span', 'normal'))
- displacement: float32 [256, 128, 1024], P('span', 'normal')
Inputs may be any that keep to these rules, and one draw needn't show every extreme that they name: In each aligned block of 2048 wall rows (rows of wall_owner taken span index first, then chord index), no owner is named by more than 32 rows; every owner is named somewhere. upstream[k, f] is -1 or a face number from f - 1024 to f - 1; upstream[0, f] = f - 1 where f >= 1.
All inputs are finite; a program needn't handle non-finite values.
Results may differ from a plain program's by a relative error of at most 0.0003.
Values sent between devices are 32-bit elements; how exact they have to be, the bound alone decides.
A program may use at most 256 MiB of HBM per device.

v0:
```python
import functools

import jax
import jax.numpy as jnp
from jax import lax
from jax.experimental import pallas as pl
from jax.experimental.pallas import tpu as pltpu
from jax.sharding import PartitionSpec as P

F32 = jnp.float32
BF16 = jnp.bfloat16
I32 = jnp.int32
MESH = pl.DeviceIdType.MESH
pseudo_step = 0.15
impact_rate = 4.0
half_step = 0.5 * pseudo_step
NX = 16
NYB = 16
NZ = 1024
LANES = 128
CH = NZ // LANES
N_SPAN = 16
N_NORMAL = 8
OWNERS = N_SPAN * N_NORMAL
SLOTS = 32
MB = 1 << 20
NT = (((1,), (1,)), ((), ()))


def iota(shape, dim):
    return lax.broadcasted_iota(I32, shape, dim)


def sweep_layer(S, V0, V1, V2, VN, NR, AIR, DRAG, emit):
    lane = iota((NYB, LANES), 1)
    row = iota((NYB, LANES), 0)
    last_lane, first_lane = lane == LANES - 1, lane == 0
    last_row, first_row = row == NYB - 1, row == 0

    def chord(c):
        zs = pl.ds(c * LANES, LANES)
        return [S(k, 0, zs) for k in range(4)] + [V2(zs)]

    here = chord(0)
    here_rolled = [pltpu.roll(t, LANES - 1, 1) for t in here]
    before = None
    for c in range(CH):
        zs = pl.ds(c * LANES, LANES)
        if c < CH - 1:
            after = chord(c + 1)
            after_rolled = [pltpu.roll(t, LANES - 1, 1) for t in after]
        else:
            after = after_rolled = [jnp.zeros((NYB, LANES), F32)] * 5
        f, v2 = here[:4], here[4]
        up = [jnp.where(last_lane, after_rolled[i], here_rolled[i]) for i in range(5)]
        w = v2 + up[4]
        pos = w > 0
        flux = [jnp.where(pos, f[k], up[k]) * w for k in range(4)]
        rolled = [pltpu.roll(t, 1, 1) for t in flux]
        if c == 0:
            edge = jnp.minimum(v2, 0.0)
            before = [edge * f[k] for k in range(4)]
        acc = [f[k] - (flux[k] - jnp.where(first_lane, before[k], rolled[k])) for k in range(4)]
        before = rolled

        v1 = V1(zs)
        w = v1 + jnp.where(last_row, VN(1, zs), pltpu.roll(v1, NYB - 1, 0))
        pos = w > 0
        w_low = VN(0, zs) + v1[0:1]
        pos_low = w_low > 0
        for k in range(4):
            upper = jnp.where(last_row, NR(1, k, zs), pltpu.roll(f[k], NYB - 1, 0))
            flux_k = jnp.where(pos, f[k], upper) * w
            low = jnp.where(pos_low, NR(0, k, zs), f[k][0:1]) * w_low
            acc[k] = acc[k] - (flux_k - jnp.where(first_row, low, pltpu.roll(flux_k, 1, 0)))

        v0 = V0(0, zs)
        w = v0 + V0(1, zs)
        w_low = V0(-1, zs) + v0
        pos, pos_low = w > 0, w_low > 0
        for k in range(4):
            flux_k = jnp.where(pos, f[k], S(k, 1, zs)) * w
            low = jnp.where(pos_low, S(k, -1, zs), f[k]) * w_low
            acc[k] = acc[k] - (flux_k - low)

        pull = pseudo_step * DRAG(zs)
        for k in range(3):
            acc[1 + k] = acc[1 + k] + pull * (f[0] * AIR(k, zs) - f[1 + k])
        emit(c, zs, acc, v0, v1, v2)
        here, here_rolled = after, after_rolled


def prep_kernel(owner_ref, face_ref, rank_ref, rank8_ref, send_ref, hq_ref):
    n = lax.axis_index("normal")
    q_len = 256
    quarters = NZ // q_len
    tri = (iota((q_len, q_len), 0) <= iota((q_len, q_len), 1)).astype(F32).astype(BF16)
    names = iota((OWNERS, q_len), 0)
    mine = N_NORMAL * iota((N_SPAN, NZ), 0) + n
    slot = iota((SLOTS, NZ), 0)
    for h in range(2):
        pieces = []
        for b in range(4):
            offset = jnp.zeros((OWNERS, 1), F32)
            got = jnp.zeros((N_SPAN, 2 * SLOTS), F32)
            for half in range(2):
                x = h * 8 + b * 2 + half
                owner = owner_ref[x]
                for q in range(quarters):
                    hot = owner[:, q * q_len : (q + 1) * q_len] == names
                    hq_ref[q * OWNERS : (q + 1) * OWNERS, :] = hot.astype(F32).astype(BF16)
                counts = jnp.dot(hq_ref[...], tri, preferred_element_type=F32)
                ranks = []
                for q in range(quarters):
                    hot = owner[:, q * q_len : (q + 1) * q_len] == names
                    part = counts[q * OWNERS : (q + 1) * OWNERS]
                    ranks.append(
                        jnp.sum(jnp.where(hot, part + offset, 0.0), axis=0, keepdims=True) - 1.0
                    )
                    offset = offset + part[:, q_len - 1 : q_len]
                rank = jnp.concatenate(ranks, axis=1).astype(I32)
                rank_ref[x] = rank
                for t in range(CH):
                    rank8_ref[x, t : t + 1, :] = rank[:, t * LANES : (t + 1) * LANES]
                face = face_ref[x : x + 1, :]
                at = slot == rank
                high = jnp.where(at, (face >> 7).astype(F32), 0.0)
                low = jnp.where(at, (face & 127).astype(F32), 0.0)
                placed = jnp.concatenate([high, low], axis=0).astype(BF16)
                hot16 = (owner == mine).astype(F32).astype(BF16)
                got = got + lax.dot_general(hot16, placed, NT, preferred_element_type=F32)
            pieces.append(got[:, :SLOTS] * 128.0 + got[:, SLOTS:])
        send_ref[:, h, :] = jnp.concatenate(pieces, axis=1).astype(I32)


def first_kernel(
    a_ref, m_ref, air_hbm, drag_hbm,
    s1_ref, v0_ref, vn_ref, nr2_ref,
    s_ref, v1_ref, v2_ref, ns_ref, nr_ref, air_ref, drag_ref,
    load_sem, air_sem, drag_sem, span_send, span_recv, normal_send, normal_recv,
):
    c, n = lax.axis_index("span"), lax.axis_index("normal")
    right, left = (c + 1) % N_SPAN, (c + N_SPAN - 1) % N_SPAN
    has_low, has_high = n > 0, n < N_NORMAL - 1

    load_a = pltpu.make_async_copy(a_ref, s_ref.at[0, pl.ds(1, NX)], load_sem.at[0])
    load_m = pltpu.make_async_copy(m_ref, s_ref.at[pl.ds(1, 3), pl.ds(1, NX)], load_sem.at[1])
    load_air = pltpu.make_async_copy(air_hbm, air_ref, air_sem)
    load_drag = pltpu.make_async_copy(drag_hbm, drag_ref, drag_sem)
    load_a.start()
    load_m.start()
    load_air.start()
    load_drag.start()

    barrier = pltpu.get_barrier_semaphore()
    for span in (left, right):
        pl.semaphore_signal(barrier, inc=1, device_id=(span, n), device_id_type=MESH)

    @pl.when(has_low)
    def _():
        pl.semaphore_signal(barrier, inc=1, device_id=(c, n - 1), device_id_type=MESH)

    @pl.when(has_high)
    def _():
        pl.semaphore_signal(barrier, inc=1, device_id=(c, n + 1), device_id_type=MESH)

    @pl.when(jnp.logical_and(has_low, has_high))
    def _():
        pl.semaphore_wait(barrier, 4)

    @pl.when(jnp.logical_not(jnp.logical_and(has_low, has_high)))
    def _():
        pl.semaphore_wait(barrier, 3)

    def span_copies(srcs, dst, base):
        copies = []
        for i, (there, layer, target) in enumerate(((right, NX, 0), (left, 1, NX + 1))):
            for j, (src, dims) in enumerate(srcs):
                copies.append(
                    pltpu.make_async_remote_copy(
                        src_ref=src(layer),
                        dst_ref=dst.at[dims, target],
                        send_sem=span_send.at[base + 2 * i + j],
                        recv_sem=span_recv.at[base + 2 * i + j],
                        device_id=(there, n),
                        device_id_type=MESH,
                    )
                )
        return copies

    def normal_copies(dst, base):
        low = pltpu.make_async_remote_copy(
            src_ref=ns_ref.at[base, 0], dst_ref=dst.at[1],
            send_sem=normal_send.at[2 * base], recv_sem=normal_recv.at[2 * base],
            device_id=(c, n - 1), device_id_type=MESH,
        )
        high = pltpu.make_async_remote_copy(
            src_ref=ns_ref.at[base, 1], dst_ref=dst.at[0],
            send_sem=normal_send.at[2 * base + 1], recv_sem=normal_recv.at[2 * base + 1],
            device_id=(c, n + 1), device_id_type=MESH,
        )
        return low, high

    def start_normal(dst, base):
        low, high = normal_copies(dst, base)

        @pl.when(has_low)
        def _():
            low.start()

        @pl.when(has_high)
        def _():
            high.start()

    def wait_normal(dst, base):
        low, high = normal_copies(dst, base)

        @pl.when(has_low)
        def _():
            low.wait_send()
            high.wait_recv()

        @pl.when(has_high)
        def _():
            high.wait_send()
            low.wait_recv()

        @pl.when(jnp.logical_not(has_low))
        def _():
            dst[0] = jnp.zeros(dst.shape[1:], F32)

        @pl.when(jnp.logical_not(has_high))
        def _():
            dst[1] = jnp.zeros(dst.shape[1:], F32)

    spans = span_copies(
        [(lambda l: a_ref.at[l - 1], 0), (lambda l: m_ref.at[:, l - 1], pl.ds(1, 3))], s_ref, 0
    )
    for copy in spans:
        copy.start()

    load_a.wait()
    load_m.wait()

    @pl.loop(0, NX)
    def _(x):
        for k in range(4):
            ns_ref[0, 0, k, x] = s_ref[k, x + 1, 0:1, :]
            ns_ref[0, 1, k, x] = s_ref[k, x + 1, NYB - 1 : NYB, :]

    start_normal(nr_ref, 0)

    @pl.loop(0, NX)
    def _(x):
        scale = half_step / s_ref[0, x + 1]
        v0_ref[x + 1] = s_ref[1, x + 1] * scale
        v1_ref[x] = s_ref[2, x + 1] * scale
        v2_ref[x] = s_ref[3, x + 1] * scale

    load_air.wait()
    load_drag.wait()
    wait_normal(nr_ref, 0)

    def edge_speed(side, present):
        @pl.when(present)
        def _():
            @pl.loop(0, NX)
            def _(x):
                vn_ref[side, x] = nr_ref[side, 2, x] * (half_step / nr_ref[side, 0, x])

        @pl.when(jnp.logical_not(present))
        def _():
            vn_ref[side] = jnp.zeros(vn_ref.shape[1:], F32)

    edge_speed(0, has_low)
    edge_speed(1, has_high)

    def layer(x):
        def emit(i, zs, acc, v0, v1, v2):
            for k in range(4):
                s1_ref[k, x, :, zs] = acc[k]
                ns_ref[1, 0, k, x - 1, :, zs] = acc[k][0:1]
                ns_ref[1, 1, k, x - 1, :, zs] = acc[k][NYB - 1 : NYB]

        sweep_layer(
            lambda k, d, zs: s_ref[k, x + d, :, zs],
            lambda d, zs: v0_ref[x + d, :, zs],
            lambda zs: v1_ref[x - 1, :, zs],
            lambda zs: v2_ref[x - 1, :, zs],
            lambda side, zs: vn_ref[side, x - 1, :, zs],
            lambda side, k, zs: nr_ref[side, k, x - 1, :, zs],
            lambda k, zs: air_ref[k, x - 1, :, zs],
            lambda zs: drag_ref[x - 1, :, zs],
            emit,
        )

    @pl.loop(0, NX)
    def _(i):
        @pl.when(i == NX - 2)
        def _():
            for copy in spans:
                copy.wait()
            for edge in (0, NX + 1):
                v0_ref[edge] = s_ref[1, edge] * (half_step / s_ref[0, edge])

        layer(jnp.where(i < NX - 2, i + 2, jnp.where(i == NX - 2, 1, NX)))

    start_normal(nr2_ref, 1)
    again = span_copies([(lambda l: s1_ref.at[:, l], pl.ds(0, 4))], s1_ref, 4)
    for copy in again:
        copy.start()
    wait_normal(nr2_ref, 1)
    for copy in again:
        copy.wait()


def second_kernel(
    sl_ref, sc_ref, su_ref, vl_ref, vc_ref, vu_ref, vn_ref, nr_ref, a_ref, m_ref, air_ref, drag_ref,
    a_out, m_out, wall_out, v1_ref, v2_ref,
):
    scale = half_step / a_ref[0]
    v1_ref[...] = m_ref[1, 0] * scale
    v2_ref[...] = m_ref[2, 0] * scale
    states = {-1: sl_ref, 0: sc_ref, 1: su_ref}
    speeds = {-1: vl_ref, 0: vc_ref, 1: vu_ref}

    def emit(i, zs, acc, v0, v1, v2):
        a_out[0, :, zs] = acc[0]
        for k in range(3):
            m_out[k, 0, :, zs] = acc[1 + k]
        catch = jnp.maximum(-acc[2][0:1], 0.0)
        s0, s1, s2 = v0[0:1], v1[0:1], v2[0:1]
        wall_out[0, 0, :, zs] = catch
        wall_out[1, 0, :, zs] = (
            catch * (0.5 / (half_step * half_step)) * (s0 * s0 + s1 * s1 + s2 * s2)
        )

    sweep_layer(
        lambda k, d, zs: states[d][k, 0, :, zs],
        lambda d, zs: speeds[d][0, :, zs],
        lambda zs: v1_ref[:, zs],
        lambda zs: v2_ref[:, zs],
        lambda side, zs: vn_ref[side, 0, :, zs],
        lambda side, k, zs: nr_ref[side, k, 0, :, zs],
        lambda k, zs: air_ref[k, 0, :, zs],
        lambda zs: drag_ref[0, :, zs],
        emit,
    )


def wall_kernel(
    wall_ref, owner_ref, owner8_ref, rank_ref, rank8_ref, sendface_ref,
    film_ref, ice_ref, cool_ref, shed_ref, share_ref, up_ref,
    film_out, ice_out, row_out,
    slots_ref, fw_ref, part_ref, got_ref, gotface_ref, lhs_ref, hot_ref, table_ref,
    links_ref, prev_ref, out_ref, back_ref, col_ref, all_ref, pick_ref,
    own_sem, sends, recvs,
):
    c, n = lax.axis_index("span"), lax.axis_index("normal")
    first_of_column, last_of_column = n == 0, n == N_NORMAL - 1
    has_next = jnp.logical_or(n < N_NORMAL - 1, c < N_SPAN - 1)
    has_prev = jnp.logical_or(n > 0, c > 0)
    next_c, next_n = jnp.where(last_of_column, c + 1, c), jnp.where(last_of_column, 0, n + 1)
    prev_c = jnp.where(first_of_column, c - 1, c)
    prev_n = jnp.where(first_of_column, N_NORMAL - 1, n - 1)
    cross_next = jnp.logical_and(last_of_column, c < N_SPAN - 1)
    cross_prev = jnp.logical_and(first_of_column, c > 0)

    barrier = pltpu.get_barrier_semaphore()

    @pl.loop(1, N_SPAN)
    def _(i):
        pl.semaphore_signal(barrier, 1, device_id=((c + i) % N_SPAN, n), device_id_type=MESH)

    @pl.loop(1, N_NORMAL)
    def _(i):
        pl.semaphore_signal(barrier, 1, device_id=(c, (n + i) % N_NORMAL), device_id_type=MESH)

    @pl.when(cross_next)
    def _():
        pl.semaphore_signal(barrier, 1, device_id=(next_c, next_n), device_id_type=MESH)

    @pl.when(cross_prev)
    def _():
        pl.semaphore_signal(barrier, 1, device_id=(prev_c, prev_n), device_id_type=MESH)

    crossing = jnp.logical_or(cross_next, cross_prev)
    peers = N_SPAN + N_NORMAL - 2

    @pl.when(crossing)
    def _():
        pl.semaphore_wait(barrier, peers + 1)

    @pl.when(jnp.logical_not(crossing))
    def _():
        pl.semaphore_wait(barrier, peers)

    def remote(src, dst, which, device):
        return pltpu.make_async_remote_copy(
            src_ref=src, dst_ref=dst, send_sem=sends.at[which], recv_sem=recvs.at[which],
            device_id=device, device_id_type=MESH,
        )

    def await_bytes(ref, sem):
        pltpu.make_async_copy(ref, ref, sem).wait()

    def to_row(src, dst, which):
        @pl.loop(1, N_SPAN)
        def _(i):
            there = (c + i) % N_SPAN
            remote(src.at[there], dst.at[c], which, (there, n)).start()

    to_row(sendface_ref, gotface_ref, 0)
    gotface_ref[c] = sendface_ref[c]

    film0 = film_ref[...]
    shed = shed_ref[...]
    out_ref[0] = film0 * shed

    @pl.when(jnp.logical_not(has_prev))
    def _():
        prev_ref[...] = jnp.zeros((2, 8, LANES), F32)

    def pass_on(step):
        return remote(out_ref.at[step], prev_ref.at[step], 1 + step, (next_c, next_n))

    @pl.when(has_next)
    def _():
        pass_on(0).start()

    for k in range(4):
        for t in range(8):
            links_ref[k, t : t + 1, :] = up_ref[k : k + 1, t * LANES : (t + 1) * LANES]
            table_ref[k, t : t + 1, :] = share_ref[k : k + 1, t * LANES : (t + 1) * LANES]

    @pl.when(first_of_column)
    def _():
        names = iota((OWNERS, NZ), 0)
        slot = iota((SLOTS, NZ), 0)

        @pl.loop(0, NX // 2)
        def _(b):
            total = jnp.zeros((4 * SLOTS, OWNERS), F32)
            for half in range(2):
                x = b * 2 + half
                owner = owner_ref[x]
                order = (owner & (N_NORMAL - 1)) * N_SPAN + (owner >> 3)
                hot = (order == names).astype(F32).astype(BF16)
                at = slot == rank_ref[x]
                rows = []
                for split in range(2):
                    for v in range(2):
                        value = wall_ref[v, x]
                        high = value.astype(BF16).astype(F32)
                        rows.append(jnp.where(at, high if split == 0 else value - high, 0.0))
                weights = jnp.concatenate(rows, axis=0).astype(BF16)
                total = total + lax.dot_general(weights, hot, NT, preferred_element_type=F32)
            both = total[: 2 * SLOTS] + total[2 * SLOTS :]
            spot = pl.ds(pl.multiple_of(b * SLOTS, SLOTS), SLOTS)
            slots_ref[0, spot, :] = both[:SLOTS]
            slots_ref[1, spot, :] = both[SLOTS:]

        for v in range(2):
            for h in range(2):
                fw_ref[:, 2 * v + h, :] = slots_ref[v, h * LANES : (h + 1) * LANES, :].T

        @pl.loop(1, N_NORMAL)
        def _(i):
            remote(fw_ref.at[pl.ds(i * N_SPAN, N_SPAN)], part_ref, 3, (c, i)).start()

        part_ref[...] = fw_ref[0:N_SPAN]

    await_bytes(gotface_ref.at[pl.ds(0, N_SPAN - 1)], recvs.at[0])
    lanes_high = iota((LANES, LANES), 0)
    for s in range(2 * N_SPAN):
        face = gotface_ref[s // 2][s % 2 : s % 2 + 1]
        hot_ref[:, s * LANES : (s + 1) * LANES] = (
            (lanes_high == (face & 127)).astype(F32).astype(BF16)
        )
        back_ref[s : s + 1, :] = face

    @pl.when(has_prev)
    def _():
        await_bytes(prev_ref.at[0], recvs.at[1])

    first_face = (c * N_NORMAL + n) * 1024

    def runin(before, own):
        total = jnp.zeros((8, LANES), F32)
        for k in range(4):
            link = links_ref[k]
            spot = link - (first_face - 1024)
            low, high = spot & 127, spot >> 7
            picked = jnp.zeros((8, LANES), F32)
            for j in range(16):
                line = before[j : j + 1] if j < 8 else own[j - 8 : j - 7]
                value = jnp.take_along_axis(
                    jnp.broadcast_to(line, (8, LANES)), low, axis=1, mode="promise_in_bounds"
                )
                picked = jnp.where(high == j, value, picked)
            total = total + table_ref[k] * jnp.where(link >= 0, picked, 0.0)
        return total

    run0 = runin(prev_ref[0], out_ref[0])

    @pl.when(jnp.logical_not(first_of_column))
    def _():
        await_bytes(part_ref, recvs.at[3])

    to_row(part_ref, got_ref, 4)
    got_ref[c] = part_ref[c]
    await_bytes(got_ref.at[pl.ds(0, N_SPAN - 1)], recvs.at[4])

    eight = iota((8, LANES), 0)
    for s in range(2 * N_SPAN):
        face_high = back_ref[s : s + 1, :] >> 7
        at = eight == face_high
        rows = []
        values = [got_ref[s // 2][2 * v + s % 2 : 2 * v + s % 2 + 1] for v in range(2)]
        highs = [value.astype(BF16).astype(F32) for value in values]
        for part in (highs, [values[v] - highs[v] for v in range(2)]):
            rows.extend(jnp.where(at, part[v], 0.0) for v in range(2))
        lhs_ref[:, s * LANES : (s + 1) * LANES] = jnp.concatenate(rows, axis=0).astype(BF16)
    sums = lax.dot_general(lhs_ref[...], hot_ref[...], NT, preferred_element_type=F32)
    sums = sums[:16] + sums[16:]
    face_catch = sums[:8]
    heat = cool_ref[...] / (1.0 + sums[8:])

    def film_step(film, outflow, run):
        inflow = impact_rate * face_catch + film - outflow + run
        frozen = heat * inflow / (heat + inflow)
        return inflow - frozen, frozen

    film1, frozen1 = film_step(film0, out_ref[0], run0)
    out_ref[1] = film1 * shed

    @pl.when(has_next)
    def _():
        pass_on(1).start()

    @pl.when(has_prev)
    def _():
        await_bytes(prev_ref.at[1], recvs.at[2])

    run1 = runin(prev_ref[1], out_ref[1])
    film2, frozen2 = film_step(film1, out_ref[1], run1)
    film_out[...] = film2
    ice2 = ice_ref[...] + frozen1 + frozen2
    ice_out[...] = ice2

    for g in range(4):
        faces = back_ref[g * 8 : g * 8 + 8, :]
        low, high = faces & 127, faces >> 7
        picked = jnp.zeros((8, LANES), F32)
        for j in range(8):
            value = jnp.take_along_axis(
                jnp.broadcast_to(ice2[j : j + 1], (8, LANES)), low, axis=1,
                mode="promise_in_bounds",
            )
            picked = jnp.where(high == j, value, picked)
        for i in range(4):
            col_ref[0, g * 4 + i] = picked[2 * i : 2 * i + 2]

    to_row(col_ref.at[0], col_ref.at[1], 5)
    col_ref[1, c] = col_ref[0, c]
    await_bytes(col_ref.at[1, pl.ds(0, N_SPAN - 1)], recvs.at[5])

    @pl.loop(1, N_NORMAL)
    def _(i):
        there = (n + i) % N_NORMAL
        remote(col_ref.at[1], all_ref.at[n], 6, (c, there)).start()

    all_ref[n] = col_ref[1]
    await_bytes(all_ref.at[pl.ds(0, N_NORMAL - 1)], recvs.at[6])

    for h in range(2):
        pick_ref[h * LANES : (h + 1) * LANES, :] = (
            all_ref[:, :, h, :].reshape(OWNERS, LANES).T
        )

    @pl.loop(0, NX)
    def _(x):
        owner = owner8_ref[x]
        order = (owner & (N_NORMAL - 1)) * N_SPAN + (owner >> 3)
        rank = rank8_ref[x]
        base = pl.multiple_of((x // 2) * SLOTS, SLOTS)
        table = pick_ref[pl.ds(base, SLOTS), :]
        picked = jnp.zeros((8, LANES), F32)
        for j in range(SLOTS):
            value = jnp.take_along_axis(
                jnp.broadcast_to(table[j : j + 1], (8, LANES)), order, axis=1,
                mode="promise_in_bounds",
            )
            picked = jnp.where(rank == j, value, picked)
        row_out[x] = picked

    await_bytes(sendface_ref.at[pl.ds(0, N_SPAN - 1)], sends.at[0])

    @pl.when(has_next)
    def _():
        await_bytes(out_ref.at[0], sends.at[1])
        await_bytes(out_ref.at[1], sends.at[2])

    @pl.when(first_of_column)
    def _():
        await_bytes(fw_ref.at[pl.ds(0, OWNERS - N_SPAN)], sends.at[3])

    await_bytes(part_ref.at[pl.ds(0, N_SPAN - 1)], sends.at[4])
    await_bytes(col_ref.at[0, pl.ds(0, N_SPAN - 1)], sends.at[5])
    await_bytes(all_ref.at[pl.ds(0, N_NORMAL - 1)], sends.at[6])


def displace_kernel(row_ref, out_ref):
    n = lax.axis_index("normal")
    y = (n * NYB + iota((NYB, LANES), 0)).astype(F32) + 0.5
    left = 1.0 - y / (NYB * N_NORMAL)
    profile = left * left
    for x in range(out_ref.shape[0]):
        for t in range(CH):
            out_ref[x, :, t * LANES : (t + 1) * LANES] = row_ref[x, t : t + 1, :] * profile


def shape(dims, dtype=F32):
    return jax.ShapeDtypeStruct(dims, dtype)


VM = pl.BlockSpec(memory_space=pltpu.VMEM)
ANY = pl.BlockSpec(memory_space=pl.ANY)


def per_device(
    volume_fraction, droplet_momentum, air_velocity, drag, wall_owner, wall_face,
    film, ice, cooling, shed, share, upstream,
):
    owner_rows = wall_owner.reshape(NX, 1, NZ)
    owner_tiles = wall_owner.reshape(NX, 8, LANES)

    rank_rows, rank_tiles, send_faces = pl.pallas_call(
        prep_kernel,
        out_shape=(
            shape((NX, 1, NZ), I32), shape((NX, 8, LANES), I32), shape((N_SPAN, 2, LANES), I32),
        ),
        in_specs=[VM] * 2,
        out_specs=(VM,) * 3,
        scratch_shapes=[pltpu.VMEM((4 * OWNERS, 256), BF16)],
        compiler_params=pltpu.CompilerParams(vmem_limit_bytes=32 * MB),
        name="slot_ranks",
    )(owner_rows, wall_face)

    brick = (NX, NYB, NZ)
    s1, v0, vn, nr2 = pl.pallas_call(
        first_kernel,
        out_shape=(
            shape((4, NX + 2, NYB, NZ)), shape((NX + 2, NYB, NZ)),
            shape((2, NX, 1, NZ)), shape((2, 4, NX, 1, NZ)),
        ),
        in_specs=[ANY] * 4,
        out_specs=(VM,) * 4,
        scratch_shapes=[
            pltpu.VMEM((4, NX + 2, NYB, NZ), F32),
            pltpu.VMEM(brick, F32),
            pltpu.VMEM(brick, F32),
            pltpu.VMEM((2, 2, 4, NX, 1, NZ), F32),
            pltpu.VMEM((2, 4, NX, 1, NZ), F32),
            pltpu.VMEM((3,) + brick, F32),
            pltpu.VMEM(brick, F32),
            pltpu.SemaphoreType.DMA((2,)),
            pltpu.SemaphoreType.DMA,
            pltpu.SemaphoreType.DMA,
            pltpu.SemaphoreType.DMA((8,)),
            pltpu.SemaphoreType.DMA((8,)),
            pltpu.SemaphoreType.DMA((4,)),
            pltpu.SemaphoreType.DMA((4,)),
        ],
        compiler_params=pltpu.CompilerParams(
            collective_id=0, has_side_effects=True, vmem_limit_bytes=48 * MB
        ),
        name="halo_sweep",
    )(volume_fraction, droplet_momentum, air_velocity, drag)

    def layers(shift):
        return pl.BlockSpec((4, 1, NYB, NZ), lambda x: (0, x + shift, 0, 0))

    def speeds(shift):
        return pl.BlockSpec((1, NYB, NZ), lambda x: (x + shift, 0, 0))

    fraction_out, momentum_out, wall = pl.pallas_call(
        second_kernel,
        out_shape=(shape(brick), shape((3,) + brick), shape((2, NX, 1, NZ))),
        grid=(NX,),
        in_specs=[layers(0), layers(1), layers(2), speeds(0), speeds(1), speeds(2),
                  pl.BlockSpec((2, 1, 1, NZ), lambda x: (0, x, 0, 0)),
                  pl.BlockSpec((2, 4, 1, 1, NZ), lambda x: (0, 0, x, 0, 0)),
                  speeds(0),
                  pl.BlockSpec((3, 1, NYB, NZ), lambda x: (0, x, 0, 0)),
                  pl.BlockSpec((3, 1, NYB, NZ), lambda x: (0, x, 0, 0)),
                  speeds(0)],
        out_specs=(speeds(0), pl.BlockSpec((3, 1, NYB, NZ), lambda x: (0, x, 0, 0)),
                   pl.BlockSpec((2, 1, 1, NZ), lambda x: (0, x, 0, 0))),
        scratch_shapes=[pltpu.VMEM((NYB, NZ), F32), pltpu.VMEM((NYB, NZ), F32)],
        compiler_params=pltpu.CompilerParams(vmem_limit_bytes=48 * MB),
        name="second_sweep",
    )(s1, s1, s1, v0, v0, v0, vn, nr2, volume_fraction, droplet_momentum, air_velocity, drag)

    tile = (8, LANES)
    film_now, ice_now, row_ice = pl.pallas_call(
        wall_kernel,
        out_shape=(shape(tile), shape(tile), shape((NX, 8, LANES))),
        in_specs=[VM] * 12,
        out_specs=(VM,) * 3,
        scratch_shapes=[
            pltpu.VMEM((2, 8 * SLOTS, OWNERS), F32),
            pltpu.VMEM((OWNERS, 4, LANES), F32),
            pltpu.VMEM((N_SPAN, 4, LANES), F32),
            pltpu.VMEM((N_SPAN, 4, LANES), F32),
            pltpu.VMEM((N_SPAN, 2, LANES), I32),
            pltpu.VMEM((32, 2 * N_SPAN * LANES), BF16),
            pltpu.VMEM((LANES, 2 * N_SPAN * LANES), BF16),
            pltpu.VMEM((4, 8, LANES), F32),
            pltpu.VMEM((4, 8, LANES), I32),
            pltpu.VMEM((2, 8, LANES), F32),
            pltpu.VMEM((2, 8, LANES), F32),
            pltpu.VMEM((2 * N_SPAN, LANES), I32),
            pltpu.VMEM((2, N_SPAN, 2, LANES), F32),
            pltpu.VMEM((N_NORMAL, N_SPAN, 2, LANES), F32),
            pltpu.VMEM((8 * SLOTS, OWNERS), F32),
            pltpu.SemaphoreType.DMA,
            pltpu.SemaphoreType.DMA((7,)),
            pltpu.SemaphoreType.DMA((7,)),
        ],
        compiler_params=pltpu.CompilerParams(
            collective_id=1, has_side_effects=True, vmem_limit_bytes=48 * MB
        ),
        name="wall_film",
    )(
        wall, owner_rows, owner_tiles, rank_rows, rank_tiles, send_faces,
        film.reshape(tile), ice.reshape(tile), cooling.reshape(tile), shed.reshape(tile),
        share, upstream,
    )

    displacement = pl.pallas_call(
        displace_kernel,
        out_shape=shape(brick),
        grid=(4,),
        in_specs=[pl.BlockSpec((NX // 4, 8, LANES), lambda i: (i, 0, 0))],
        out_specs=pl.BlockSpec((NX // 4, NYB, NZ), lambda i: (i, 0, 0)),
        name="displace",
    )(row_ice)
    return fraction_out, momentum_out, film_now.reshape(-1), ice_now.reshape(-1), displacement


def solution(mesh):
    volume = P("span", "normal", None)
    vector = P(None, "span", "normal", None)
    faces = P(("span", "normal"))
    links = P(None, ("span", "normal"))
    return jax.shard_map(
        per_device,
        mesh=mesh,
        in_specs=(
            volume, vector, vector, volume, P("span", None, None), P("span", None),
            faces, faces, faces, faces, links, links,
        ),
        out_specs=(volume, vector, faces, faces, volume),
        check_vma=False,
    )
```

profile of v0, /device:TPU:1, one launch (start us, length us, event | category | flops | bytes accessed | tf_op | source)
XLA Modules:
  0.0 83.6 jit_solution(18350154025410405836)
XLA Ops:
  0.6 0.0 copy-start
  0.6 1.2 %copy-done = f32[16,16,1024]{2,1,0:T(8,128)S(1)} copy-done((f32[16,16,1024]{2,1,0:T(8,128)S(1)}, f32[16,16,1024]{2,1,0:T(8,128)}, u32[]{:S(2)}) %copy-start) | copy-done | bytes 1048600
  1.9 0.0 copy-start.1
  1.9 1.2 %copy-done.1 = f32[16,16,1024]{2,1,0:T(8,128)S(1)} copy-done((f32[16,16,1024]{2,1,0:T(8,128)S(1)}, f32[16,16,1024]{2,1,0:T(8,128)}, u32[]{:S(2)}) %copy-start.1) | copy-done | bytes 1048600
  3.1 29.2 %halo_sweep.1 = (f32[4,18,16,1024]{3,2,1,0:T(8,128)}, f32[18,16,1024]{2,1,0:T(8,128)S(1)}, f32[2,16,1,1024]{3,2,1,0:T(1,128)S(1)}, f32[2,4,16,1,1024]{4,3,2,1,0:T(1,128)S(1)}) custom-call(f32[16,16,1024]{2,1,0:T(8,128)S(1)} %copy-done, f32[3,16,16,1024]{3,2,1,0:T(8,128)} %m_ref.3, f32[3,16,16,1024]{3,2,1,0:T(8,128)} %air_ref.1, f32[16,16,1024]{2,1,0:T(8,128)S(1)} %copy-done.1), custom_call_target="tpu_custom_call" | custom-call | tf_op jit(solution)/shard_map/halo_sweep/pallas_call | solution.py:651
  32.3 0.0 copy-start.2
  32.3 0.0 copy-start.4
  32.3 0.0 copy-start.5
  32.3 0.0 copy-start.6
  32.3 0.0 copy-start.7
  32.3 0.0 copy-start.8
  32.3 0.0 copy-start.9
  32.3 0.0 copy-start.10
  32.4 15.5 %second_sweep.1 = (f32[16,16,1024]{2,1,0:T(8,128)}, f32[3,16,16,1024]{3,2,1,0:T(8,128)}, f32[2,16,1,1024]{3,2,1,0:T(1,128)S(1)}) custom-call(f32[4,18,16,1024]{3,2,1,0:T(8,128)} %get-tuple-element.18.sl_ref.sc_ref.su_ref, f32[4,18,16,1024]{3,2,1,0:T(8,128)} %get-tuple-element.18.sl_ref.sc_ref.su_ref, ...), custom_call_target="tpu_custom_call" | custom-call | tf_op jit(solution)/shard_map/second_sweep/pallas_call | solution.py:687
  47.8 0.0 copy-done.2
  47.8 0.0 copy-done.4
  47.8 3.5 %slot_ranks.1 = (s32[16,1,1024]{2,1,0:T(1,128)S(1)}, s32[16,8,128]{2,1,0:T(8,128)S(1)}, s32[16,2,128]{2,1,0:T(2,128)S(1)}) custom-call(s32[16,1,1024]{2,1,0:T(1,128)S(1)} %bitcast.8, s32[16,1024]{1,0:T(8,128)S(1)} %copy-done.4), custom_call_target="tpu_custom_call" | custom-call | tf_op jit(solution)/shard_map/slot_ranks/pallas_call | solution.py:638
  51.4 0.0 copy-done.5
  51.4 0.0 copy-done.6
  51.4 0.0 copy-done.7
  51.4 0.0 copy-done.8
  51.4 0.0 copy-done.9
  51.4 0.0 copy-done.10
  51.4 27.5 %wall_film.1 = (f32[8,128]{1,0:T(8,128)S(1)}, f32[8,128]{1,0:T(8,128)S(1)}, f32[16,8,128]{2,1,0:T(8,128)S(1)}) custom-call(f32[2,16,1,1024]{3,2,1,0:T(1,128)S(1)} %get-tuple-element.24.wall_ref, s32[16,1,1024]{2,1,0:T(1,128)S(1)} %bitcast.9, s32[16,8,128]{2,1,0:T(8,128)S(1)} %bitcast.10, s32[16,1,1024]{2,1,0:T(1,128)S(1)} %get-tuple-element.25.rank_ref, ...), custom_call_target="tpu_custom_call" | custom-call | tf_op jit(solution)/shard_map/wall_film/pallas_call | solution.py:706
  78.9 0.0 copy-start.3
  79.0 0.6 copy-done.3
  79.6 2.9 %displace.1 = f32[16,16,1024]{2,1,0:T(8,128)} custom-call(f32[16,8,128]{2,1,0:T(8,128)} %copy-done.3), custom_call_target="tpu_custom_call" | custom-call | tf_op jit(solution)/shard_map/displace/pallas_call | solution.py:741
  82.5 0.6 copy.19
  83.1 0.6 copy.20
Async XLA Ops:
  0.6 1.2 %copy-start = (f32[16,16,1024]{2,1,0:T(8,128)S(1)}, f32[16,16,1024]{2,1,0:T(8,128)}, u32[]{:S(2)}) copy-start(f32[16,16,1024]{2,1,0:T(8,128)} %a_ref.3) | copy-start | bytes 3145732
  1.9 1.2 %copy-start.1 = (f32[16,16,1024]{2,1,0:T(8,128)S(1)}, f32[16,16,1024]{2,1,0:T(8,128)}, u32[]{:S(2)}) copy-start(f32[16,16,1024]{2,1,0:T(8,128)} %drag_ref.1) | copy-start | bytes 3145732
  32.3 15.6 %copy-start.2 = (s32[16,1024,1]{1,2,0:T(1,128)S(1)}, s32[16,1024,1]{1,2,0:T(1,128)}, u32[]{:S(2)}) copy-start(s32[16,1024,1]{1,2,0:T(1,128)} %param.16) | copy-start | bytes 196612
  32.3 15.6 %copy-start.4 = (s32[16,1024]{1,0:T(8,128)S(1)}, s32[16,1024]{1,0:T(8,128)}, u32[]{:S(2)}) copy-start(s32[16,1024]{1,0:T(8,128)} %face_ref.1) | copy-start | bytes 196612
  32.3 19.1 %copy-start.5 = (f32[4,1024]{1,0:T(4,128)S(1)}, f32[4,1024]{1,0:T(4,128)}, u32[]{:S(2)}) copy-start(f32[4,1024]{1,0:T(4,128)} %share_ref.1) | copy-start | bytes 49156
  32.3 19.1 %copy-start.6 = (s32[4,1024]{1,0:T(4,128)S(1)}, s32[4,1024]{1,0:T(4,128)}, u32[]{:S(2)}) copy-start(s32[4,1024]{1,0:T(4,128)} %up_ref.1) | copy-start | bytes 49156
  32.3 19.1 %copy-start.7 = (f32[1024]{0:T(1024)S(1)}, f32[1024]{0:T(1024)}, u32[]{:S(2)}) copy-start(f32[1024]{0:T(1024)} %param.18) | copy-start | bytes 12292
  32.3 19.1 %copy-start.8 = (f32[1024]{0:T(1024)S(1)}, f32[1024]{0:T(1024)}, u32[]{:S(2)}) copy-start(f32[1024]{0:T(1024)} %param.19) | copy-start | bytes 12292
  32.3 19.1 %copy-start.9 = (f32[1024]{0:T(1024)S(1)}, f32[1024]{0:T(1024)}, u32[]{:S(2)}) copy-start(f32[1024]{0:T(1024)} %param.20) | copy-start | bytes 12292
  32.3 19.1 %copy-start.10 = (f32[1024]{0:T(1024)S(1)}, f32[1024]{0:T(1024)}, u32[]{:S(2)}) copy-start(f32[1024]{0:T(1024)} %param.21) | copy-start | bytes 12292
  78.9 0.6 copy-start.3
where the time goes:
time: 84.4 us; the launch traced here: 83.6 us
  Pallas kernels  78.6 us (93%)
  local copies, waits for them, and re-layouts  4.29 us (5%)
    pallas_call x1, Pallas kernels, per_device(): pl.pallas_call(first_kernel, out_shape=(shape((4, NX + 2, NYB, NZ)), shap...  29.2 us
    pallas_call x1, Pallas kernels, per_device(): pl.pallas_call(wall_kernel, out_shape=(shape(tile), shape(tile), shape((N...  27.5 us
    pallas_call x1, Pallas kernels, per_device(): pl.pallas_call(second_kernel, out_shape=(shape(brick), shape((3,) + brick...  15.5 us
    unnamed x24, local copies, waits for them, and re-layouts  4.29 us
    pallas_call x1, Pallas kernels, per_device(): pl.pallas_call(prep_kernel, out_shape=(shape((NX, 1, NZ), I32), shape((NX...  3.53 us
    pallas_call x1, Pallas kernels, per_device(): pl.pallas_call(displace_kernel, out_shape=shape(brick), grid=(4,), in_spe...  2.9 us

commit v1 on v0

v1 whole, which is shorter than its diff:
```python
import functools

import jax
import jax.numpy as jnp
from jax import lax
from jax.experimental import pallas as pl
from jax.experimental.pallas import tpu as pltpu
from jax.sharding import PartitionSpec as P

F32 = jnp.float32
BF16 = jnp.bfloat16
I32 = jnp.int32
MESH = pl.DeviceIdType.MESH
pseudo_step = 0.15
impact_rate = 4.0
half_step = 0.5 * pseudo_step
NX = 16
NYB = 16
NZ = 1024
LANES = 128
CH = NZ // LANES
N_SPAN = 16
N_NORMAL = 8
OWNERS = N_SPAN * N_NORMAL
SLOTS = 32
MB = 1 << 20
NT = (((1,), (1,)), ((), ()))


def iota(shape, dim):
    return lax.broadcasted_iota(I32, shape, dim)


def sweep_layer(S, V0, V1, V2, VN, NR, AIR, DRAG, emit):
    lane = iota((NYB, LANES), 1)
    row = iota((NYB, LANES), 0)
    last_lane, first_lane = lane == LANES - 1, lane == 0
    last_row, first_row = row == NYB - 1, row == 0

    def chord(c):
        zs = pl.ds(c * LANES, LANES)
        return [S(k, 0, zs) for k in range(4)] + [V2(zs)]

    here = chord(0)
    here_rolled = [pltpu.roll(t, LANES - 1, 1) for t in here]
    before = None
    for c in range(CH):
        zs = pl.ds(c * LANES, LANES)
        if c < CH - 1:
            after = chord(c + 1)
            after_rolled = [pltpu.roll(t, LANES - 1, 1) for t in after]
        else:
            after = after_rolled = [jnp.zeros((NYB, LANES), F32)] * 5
        f, v2 = here[:4], here[4]
        up = [jnp.where(last_lane, after_rolled[i], here_rolled[i]) for i in range(5)]
        w = v2 + up[4]
        pos = w > 0
        flux = [jnp.where(pos, f[k], up[k]) * w for k in range(4)]
        rolled = [pltpu.roll(t, 1, 1) for t in flux]
        if c == 0:
            edge = jnp.minimum(v2, 0.0)
            before = [edge * f[k] for k in range(4)]
        acc = [f[k] - (flux[k] - jnp.where(first_lane, before[k], rolled[k])) for k in range(4)]
        before = rolled

        v1 = V1(zs)
        w = v1 + jnp.where(last_row, VN(1, zs), pltpu.roll(v1, NYB - 1, 0))
        pos = w > 0
        w_low = VN(0, zs) + v1[0:1]
        pos_low = w_low > 0
        for k in range(4):
            upper = jnp.where(last_row, NR(1, k, zs), pltpu.roll(f[k], NYB - 1, 0))
            flux_k = jnp.where(pos, f[k], upper) * w
            low = jnp.where(pos_low, NR(0, k, zs), f[k][0:1]) * w_low
            acc[k] = acc[k] - (flux_k - jnp.where(first_row, low, pltpu.roll(flux_k, 1, 0)))

        v0 = V0(0, zs)
        w = v0 + V0(1, zs)
        w_low = V0(-1, zs) + v0
        pos, pos_low = w > 0, w_low > 0
        for k in range(4):
            flux_k = jnp.where(pos, f[k], S(k, 1, zs)) * w
            low = jnp.where(pos_low, S(k, -1, zs), f[k]) * w_low
            acc[k] = acc[k] - (flux_k - low)

        pull = pseudo_step * DRAG(zs)
        for k in range(3):
            acc[1 + k] = acc[1 + k] + pull * (f[0] * AIR(k, zs) - f[1 + k])
        emit(c, zs, acc, v0, v1, v2)
        here, here_rolled = after, after_rolled


def advance(S, V0, V1, V2, VN, NR, AIR, DRAG, emit, x):
    sweep_layer(
        lambda k, d, zs: S[k, x + d, :, zs],
        lambda d, zs: V0[x + d, :, zs],
        lambda zs: V1[x - 1, :, zs],
        lambda zs: V2[x - 1, :, zs],
        lambda side, zs: VN[side, x - 1, :, zs],
        lambda side, k, zs: NR[side, k, x - 1, :, zs],
        lambda k, zs: AIR[k, x - 1, :, zs],
        lambda zs: DRAG[x - 1, :, zs],
        emit,
    )


def layer_of(i):
    return jnp.where(i < NX - 2, i + 2, jnp.where(i == NX - 2, 1, NX))


def prepare(owner_ref, face_ref, rank_ref, key8_ref, send_ref, hot_ref, n):
    q_len = 256
    quarters = NZ // q_len
    tri = (iota((q_len, q_len), 0) <= iota((q_len, q_len), 1)).astype(F32).astype(BF16)
    names = iota((OWNERS, q_len), 0)
    mine = n * N_SPAN + iota((N_SPAN, NZ), 0)
    slot = iota((SLOTS, NZ), 0)
    for h in range(2):
        pieces = []
        for b in range(4):
            offset = jnp.zeros((OWNERS, 1), F32)
            got = jnp.zeros((N_SPAN, 2 * SLOTS), F32)
            for half in range(2):
                x = h * 8 + b * 2 + half
                owner = owner_ref[x]
                order = (owner & (N_NORMAL - 1)) * N_SPAN + (owner >> 3)
                hots = []
                for q in range(quarters):
                    qs = slice(q * q_len, (q + 1) * q_len)
                    hot = (order[:, qs] == names).astype(F32).astype(BF16)
                    hot_ref[x, :, qs] = hot
                    hots.append(hot)
                counts = jnp.dot(
                    jnp.concatenate(hots, axis=0), tri, preferred_element_type=F32
                )
                ranks = []
                for q in range(quarters):
                    hot = order[:, q * q_len : (q + 1) * q_len] == names
                    part = counts[q * OWNERS : (q + 1) * OWNERS]
                    ranks.append(
                        jnp.sum(jnp.where(hot, part + offset, 0.0), axis=0, keepdims=True) - 1.0
                    )
                    offset = offset + part[:, q_len - 1 : q_len]
                rank = jnp.concatenate(ranks, axis=1).astype(I32)
                rank_ref[x] = rank
                key = order * SLOTS + rank
                for t in range(CH):
                    key8_ref[x, t : t + 1, :] = key[:, t * LANES : (t + 1) * LANES]
                face = face_ref[x : x + 1, :]
                at = slot == rank
                high = jnp.where(at, (face >> 7).astype(F32), 0.0)
                low = jnp.where(at, (face & 127).astype(F32), 0.0)
                placed = jnp.concatenate([high, low], axis=0).astype(BF16)
                hot16 = (order == mine).astype(F32).astype(BF16)
                got = got + lax.dot_general(hot16, placed, NT, preferred_element_type=F32)
            pieces.append(got[:, :SLOTS] * 128.0 + got[:, SLOTS:])
        send_ref[:, h, :] = jnp.concatenate(pieces, axis=1).astype(I32)


PR = 24
FR = (0, 1, 2)
MS = (3, 4)
MN = (5, 6, 7)
MC = (8, 9)
AN = (10, 11)
DR = (12, 13)
NEAR = (0, 1, 3, 4, 5, 6, 8, 10, 12)
FAR = (0, 3, 5)
STRIP = len(NEAR) + len(FAR)


def flux_of(w, low, high):
    return jnp.where(w > 0, low, high) * w


def wall_strip(pk, vq, q1, wv):
    lane = iota((PR, LANES), 1)
    last_lane, first_lane = lane == LANES - 1, lane == 0

    def tile(ref, i, t):
        return ref[i, :, t * LANES : (t + 1) * LANES]

    def next_tile(ref, i, t):
        here = pltpu.roll(tile(ref, i, t), LANES - 1, 1)
        if t == CH - 1:
            return jnp.where(last_lane, 0.0, here)
        return jnp.where(last_lane, pltpu.roll(tile(ref, i, t + 1), LANES - 1, 1), here)

    def spanwise(f, v):
        flux = flux_of(v + pltpu.roll(v, PR - 1, 0), f, pltpu.roll(f, PR - 1, 0))
        return flux - pltpu.roll(flux, 1, 0)

    def chordwise(ref, i, f, v, v_next, t, before):
        flux = flux_of(v + v_next, f, next_tile(ref, i, t))
        rolled = pltpu.roll(flux, 1, 1)
        if t == 0:
            before = jnp.minimum(v, 0.0) * f
        return flux - jnp.where(first_lane, before, rolled), rolled

    for y in range(3):
        for t in range(CH):
            zs = slice(t * LANES, (t + 1) * LANES)
            scale = half_step / tile(pk, FR[y], t)
            vq[2 + y, :, zs] = tile(pk, MN[y], t) * scale
            if y < 2:
                vq[y, :, zs] = tile(pk, MS[y], t) * scale
                vq[5 + y, :, zs] = tile(pk, MC[y], t) * scale

    before = [None] * 3
    for t in range(CH):
        zs = slice(t * LANES, (t + 1) * LANES)
        v0, v0_1 = tile(vq, 0, t), tile(vq, 1, t)
        v1, v1_1, v1_2 = tile(vq, 2, t), tile(vq, 3, t), tile(vq, 4, t)
        v2, v2_1 = tile(vq, 5, t), tile(vq, 6, t)
        v2_next, v2_1_next = next_tile(vq, 5, t), next_tile(vq, 6, t)
        a0, a1 = tile(pk, FR[0], t), tile(pk, FR[1], t)
        m0, m1, m2 = (tile(pk, i, t) for i in MN)
        w0, w1 = v1 + v1_1, v1_1 + v1_2
        wall = jnp.minimum(v1, 0.0)
        along, before[0] = chordwise(pk, FR[0], a0, v2, v2_next, t, before[0])
        q1[0, :, zs] = (
            a0 - along - spanwise(a0, v0) - (flux_of(w0, a0, a1) - wall * a0)
        )
        between = flux_of(w0, m0, m1)
        along, before[1] = chordwise(pk, MN[0], m0, v2, v2_next, t, before[1])
        q1[1, :, zs] = (
            m0 - along - spanwise(m0, v0) - (between - wall * m0)
            + pseudo_step * tile(pk, DR[0], t) * (a0 * tile(pk, AN[0], t) - m0)
        )
        along, before[2] = chordwise(pk, MN[1], m1, v2_1, v2_1_next, t, before[2])
        q1[2, :, zs] = (
            m1 - along - spanwise(m1, v0_1) - (flux_of(w1, m1, m2) - between)
            + pseudo_step * tile(pk, DR[1], t) * (a1 * tile(pk, AN[1], t) - m1)
        )

    before = None
    for t in range(CH):
        zs = slice(t * LANES, (t + 1) * LANES)
        v0, v1, v1_1, v2 = (tile(vq, i, t) for i in (0, 2, 3, 5))
        a0, m0, m1 = (tile(q1, i, t) for i in range(3))
        along, before = chordwise(q1, 1, m0, v2, next_tile(vq, 5, t), t, before)
        out = (
            m0 - along - spanwise(m0, v0)
            - (flux_of(v1 + v1_1, m0, m1) - jnp.minimum(v1, 0.0) * m0)
            + pseudo_step * tile(pk, DR[0], t) * (a0 * tile(pk, AN[0], t) - m0)
        )
        catch = jnp.maximum(-out, 0.0)
        wv[0, :, zs] = catch
        wv[1, :, zs] = (
            catch * (0.5 / (half_step * half_step)) * (v0 * v0 + v1 * v1 + v2 * v2)
        )


def main_kernel(
    a_hbm, m_hbm, air_hbm, drag_hbm, owner_hbm, face_hbm,
    film_hbm, ice_hbm, cool_hbm, shed_hbm, share_hbm, up_hbm,
    frac_out, mom_out, film_out, ice_out, all_ref, key8_ref,
    owner_ref, face_ref, film_ref, ice_ref, cool_ref, shed_ref, share_ref, up_ref,
    s_ref, s1_ref, v0_ref, v1_ref, v2_ref, vn_ref, ns_ref, nr_ref, nr2_ref, air_ref, drag_ref,
    owner_hot, rank_ref, sendface_ref, pk, vq, q1, wv, strip_out, strip_in,
    slots_ref, fw_ref, part_ref, got_ref, gotface_ref, lhs_ref, hot_ref,
    links_ref, weight_ref, prev_ref, out_ref, back_ref, col_ref,
    load_sem, small_sem, span_send, span_recv, normal_send, normal_recv, strip_send, strip_recv, sends, recvs,
):
    c, n = lax.axis_index("span"), lax.axis_index("normal")
    right, left = (c + 1) % N_SPAN, (c + N_SPAN - 1) % N_SPAN
    on_wall, has_low, has_high = n == 0, n > 0, n < N_NORMAL - 1
    off_wall = has_low
    last_of_column = n == N_NORMAL - 1
    has_next = jnp.logical_or(has_high, c < N_SPAN - 1)
    has_prev = jnp.logical_or(has_low, c > 0)
    next_c, next_n = jnp.where(last_of_column, c + 1, c), jnp.where(last_of_column, 0, n + 1)
    prev_c, prev_n = jnp.where(on_wall, c - 1, c), jnp.where(on_wall, N_NORMAL - 1, n - 1)
    cross_next = jnp.logical_and(last_of_column, c < N_SPAN - 1)
    cross_prev = jnp.logical_and(on_wall, c > 0)

    first_loads = [
        pltpu.make_async_copy(src, dst, small_sem.at[i])
        for i, (src, dst) in enumerate(((owner_hbm, owner_ref), (face_hbm, face_ref)))
    ]
    loads = [
        pltpu.make_async_copy(a_hbm, s_ref.at[0, pl.ds(1, NX)], load_sem.at[0]),
        pltpu.make_async_copy(m_hbm, s_ref.at[pl.ds(1, 3), pl.ds(1, NX)], load_sem.at[1]),
        pltpu.make_async_copy(air_hbm, air_ref, load_sem.at[2]),
        pltpu.make_async_copy(drag_hbm, drag_ref, load_sem.at[3]),
    ] + [
        pltpu.make_async_copy(src, dst, small_sem.at[2 + i])
        for i, (src, dst) in enumerate(
            ((film_hbm, film_ref), (ice_hbm, ice_ref), (cool_hbm, cool_ref), (shed_hbm, shed_ref),
             (share_hbm, share_ref), (up_hbm, up_ref))
        )
    ]
    for load in first_loads + loads:
        load.start()

    barrier = pltpu.get_barrier_semaphore()

    @pl.loop(1, N_SPAN)
    def _(i):
        pl.semaphore_signal(barrier, 1, device_id=((c + i) % N_SPAN, n), device_id_type=MESH)

    @pl.loop(1, N_NORMAL)
    def _(i):
        pl.semaphore_signal(barrier, 1, device_id=(c, (n + i) % N_NORMAL), device_id_type=MESH)

    @pl.when(cross_next)
    def _():
        pl.semaphore_signal(barrier, 1, device_id=(next_c, next_n), device_id_type=MESH)

    @pl.when(cross_prev)
    def _():
        pl.semaphore_signal(barrier, 1, device_id=(prev_c, prev_n), device_id_type=MESH)

    for load in first_loads:
        load.wait()
    prepare(owner_ref, face_ref, rank_ref, key8_ref, sendface_ref, owner_hot, n)
    for load in loads:
        load.wait()

    @pl.when(on_wall)
    def _():
        for i in range(14):
            pk[i, 0:8, :] = jnp.ones((8, NZ), F32)
            pk[i, 16:24, :] = jnp.ones((8, NZ), F32)
        for x in range(NX):
            at = slice(x + 2, x + 3)
            for y in range(3):
                pk[FR[y], at, :] = s_ref[0, x + 1, y : y + 1, :]
                pk[MN[y], at, :] = s_ref[2, x + 1, y : y + 1, :]
                if y < 2:
                    pk[MS[y], at, :] = s_ref[1, x + 1, y : y + 1, :]
                    pk[MC[y], at, :] = s_ref[3, x + 1, y : y + 1, :]
                    pk[AN[y], at, :] = air_ref[1, x, y : y + 1, :]
                    pk[DR[y], at, :] = drag_ref[x, y : y + 1, :]
        for side, near, far in ((0, NX - 1, NX - 2), (1, 0, 1)):
            for j, i in enumerate(NEAR):
                strip_out[side, j] = pk[i, near + 2 : near + 3, :]
            for j, i in enumerate(FAR):
                strip_out[side, len(NEAR) + j] = pk[i, far + 2 : far + 3, :]

    @pl.loop(0, NX)
    def _(x):
        for k in range(4):
            ns_ref[0, 0, k, x] = s_ref[k, x + 1, 0:1, :]
            ns_ref[0, 1, k, x] = s_ref[k, x + 1, NYB - 1 : NYB, :]

    film0 = film_ref[...]
    shed = shed_ref[...]
    out_ref[0] = film0 * shed

    @pl.when(jnp.logical_not(has_prev))
    def _():
        prev_ref[...] = jnp.zeros((2, 8, LANES), F32)

    crossing = jnp.logical_or(cross_next, cross_prev)
    peers = N_SPAN + N_NORMAL - 2

    @pl.when(crossing)
    def _():
        pl.semaphore_wait(barrier, peers + 1)

    @pl.when(jnp.logical_not(crossing))
    def _():
        pl.semaphore_wait(barrier, peers)

    def remote(src, dst, send, recv, device):
        return pltpu.make_async_remote_copy(
            src_ref=src, dst_ref=dst, send_sem=send, recv_sem=recv,
            device_id=device, device_id_type=MESH,
        )

    def await_bytes(ref, sem):
        pltpu.make_async_copy(ref, ref, sem).wait()

    def to_row(src, dst, which):
        @pl.loop(1, N_SPAN)
        def _(i):
            there = (c + i) % N_SPAN
            remote(src.at[there], dst.at[c], sends.at[which], recvs.at[which], (there, n)).start()

    strips = [
        remote(
            strip_out.at[side], strip_in.at[side], strip_send.at[side], strip_recv.at[side],
            (there, n),
        )
        for side, there in ((0, right), (1, left))
    ]

    @pl.when(on_wall)
    def _():
        for copy in strips:
            copy.start()

    def normal_copies(base, dst):
        return (
            remote(ns_ref.at[base, 0], dst.at[1], normal_send.at[2 * base],
                   normal_recv.at[2 * base], (c, n - 1)),
            remote(ns_ref.at[base, 1], dst.at[0], normal_send.at[2 * base + 1],
                   normal_recv.at[2 * base + 1], (c, n + 1)),
        )

    def start_normal(base, dst):
        low, high = normal_copies(base, dst)

        @pl.when(has_low)
        def _():
            low.start()

        @pl.when(has_high)
        def _():
            high.start()

    def wait_normal(base, dst):
        low, high = normal_copies(base, dst)

        @pl.when(has_low)
        def _():
            low.wait_send()
            high.wait_recv()

        @pl.when(has_high)
        def _():
            high.wait_send()
            low.wait_recv()

        @pl.when(jnp.logical_not(has_low))
        def _():
            dst[0] = jnp.zeros(dst.shape[1:], F32)

        @pl.when(jnp.logical_not(has_high))
        def _():
            dst[1] = jnp.zeros(dst.shape[1:], F32)

    def span_copies(src, dst, base):
        return [
            remote(src.at[:, layer], dst.at[:, target], span_send.at[base + i],
                   span_recv.at[base + i], (there, n))
            for i, (there, layer, target) in enumerate(((right, NX, 0), (left, 1, NX + 1)))
        ]

    start_normal(0, nr_ref)
    to_row(sendface_ref, gotface_ref, 0)
    gotface_ref[c] = sendface_ref[c]

    def pass_on(step):
        return remote(out_ref.at[step], prev_ref.at[step], sends.at[1 + step],
                      recvs.at[1 + step], (next_c, next_n))

    @pl.when(has_next)
    def _():
        pass_on(0).start()

    spans = span_copies(s_ref, s_ref, 0)
    for copy in spans:
        copy.start()

    @pl.when(on_wall)
    def _():
        for copy in strips:
            copy.wait()
        for side, near, far in ((0, 1, 0), (1, NX + 2, NX + 3)):
            for j, i in enumerate(NEAR):
                pk[i, near : near + 1, :] = strip_in[side, j]
            for j, i in enumerate(FAR):
                pk[i, far : far + 1, :] = strip_in[side, len(NEAR) + j]
        wall_strip(pk, vq, q1, wv)
        slot = iota((SLOTS, NZ), 0)

        @pl.loop(0, NX // 2)
        def _(b):
            total = jnp.zeros((4 * SLOTS, OWNERS), F32)
            for half in range(2):
                x = b * 2 + half
                at = slot == rank_ref[x]
                rows = []
                for split in range(2):
                    for v in range(2):
                        value = wv[v, pl.ds(x + 2, 1), :]
                        high = value.astype(BF16).astype(F32)
                        rows.append(jnp.where(at, high if split == 0 else value - high, 0.0))
                weights = jnp.concatenate(rows, axis=0).astype(BF16)
                total = total + lax.dot_general(
                    weights, owner_hot[x], NT, preferred_element_type=F32
                )
            both = total[: 2 * SLOTS] + total[2 * SLOTS :]
            spot = pl.ds(pl.multiple_of(b * SLOTS, SLOTS), SLOTS)
            slots_ref[0, spot, :] = both[:SLOTS]
            slots_ref[1, spot, :] = both[SLOTS:]

        for v in range(2):
            for h in range(2):
                fw_ref[:, 2 * v + h, :] = slots_ref[v, h * LANES : (h + 1) * LANES, :].T

        @pl.loop(1, N_NORMAL)
        def _(i):
            remote(fw_ref.at[pl.ds(i * N_SPAN, N_SPAN)], part_ref, sends.at[3], recvs.at[3],
                   (c, i)).start()

        part_ref[...] = fw_ref[0:N_SPAN]
        to_row(part_ref, got_ref, 4)

    @pl.loop(0, NX)
    def _(x):
        scale = half_step / s_ref[0, x + 1]
        v0_ref[x + 1] = s_ref[1, x + 1] * scale
        v1_ref[x] = s_ref[2, x + 1] * scale
        v2_ref[x] = s_ref[3, x + 1] * scale

    for k in range(4):
        for t in range(8):
            links_ref[k, t : t + 1, :] = up_ref[k : k + 1, t * LANES : (t + 1) * LANES]
            weight_ref[k, t : t + 1, :] = share_ref[k : k + 1, t * LANES : (t + 1) * LANES]
    await_bytes(gotface_ref.at[pl.ds(0, N_SPAN - 1)], recvs.at[0])
    lanes_high = iota((LANES, LANES), 0)
    for s in range(2 * N_SPAN):
        face = gotface_ref[s // 2][s % 2 : s % 2 + 1]
        hot_ref[:, s * LANES : (s + 1) * LANES] = (
            (lanes_high == (face & 127)).astype(F32).astype(BF16)
        )
        back_ref[s : s + 1, :] = face

    @pl.when(has_prev)
    def _():
        await_bytes(prev_ref.at[0], recvs.at[1])

    first_face = (c * N_NORMAL + n) * 1024

    def runin(before, own):
        total = jnp.zeros((8, LANES), F32)
        for k in range(4):
            link = links_ref[k]
            spot = link - (first_face - 1024)
            low, high = spot & 127, spot >> 7
            picked = jnp.zeros((8, LANES), F32)
            for j in range(16):
                line = before[j : j + 1] if j < 8 else own[j - 8 : j - 7]
                value = jnp.take_along_axis(
                    jnp.broadcast_to(line, (8, LANES)), low, axis=1, mode="promise_in_bounds"
                )
                picked = jnp.where(high == j, value, picked)
            total = total + weight_ref[k] * jnp.where(link >= 0, picked, 0.0)
        return total

    run0 = runin(prev_ref[0], out_ref[0])

    wait_normal(0, nr_ref)

    def edge_speed(side, present):
        @pl.when(present)
        def _():
            @pl.loop(0, NX)
            def _(x):
                vn_ref[side, x] = nr_ref[side, 2, x] * (half_step / nr_ref[side, 0, x])

        @pl.when(jnp.logical_not(present))
        def _():
            vn_ref[side] = jnp.zeros(vn_ref.shape[1:], F32)

    edge_speed(0, has_low)
    edge_speed(1, has_high)

    def first_layer(i):
        x = layer_of(i)

        def emit(t, zs, acc, v0, v1, v2):
            for k in range(4):
                s1_ref[k, x, :, zs] = acc[k]
                ns_ref[1, 0, k, x - 1, :, zs] = acc[k][0:1]
                ns_ref[1, 1, k, x - 1, :, zs] = acc[k][NYB - 1 : NYB]

        advance(s_ref, v0_ref, v1_ref, v2_ref, vn_ref, nr_ref, air_ref, drag_ref, emit, x)

    @pl.loop(0, FIRST_CUT)
    def _(i):
        first_layer(i)

    @pl.when(off_wall)
    def _():
        await_bytes(part_ref, recvs.at[3])
        to_row(part_ref, got_ref, 4)

    got_ref[c] = part_ref[c]

    @pl.loop(FIRST_CUT, NX)
    def _(i):
        @pl.when(i == NX - 2)
        def _():
            for copy in spans:
                copy.wait()
            for edge in (0, NX + 1):
                v0_ref[edge] = s_ref[1, edge] * (half_step / s_ref[0, edge])

        first_layer(i)

    start_normal(1, nr2_ref)
    again = span_copies(s1_ref, s1_ref, 2)
    for copy in again:
        copy.start()

    await_bytes(got_ref.at[pl.ds(0, N_SPAN - 1)], recvs.at[4])
    eight = iota((8, LANES), 0)
    for s in range(2 * N_SPAN):
        at = eight == (back_ref[s : s + 1, :] >> 7)
        values = [got_ref[s // 2][2 * v + s % 2 : 2 * v + s % 2 + 1] for v in range(2)]
        highs = [value.astype(BF16).astype(F32) for value in values]
        rows = []
        for part in (highs, [values[v] - highs[v] for v in range(2)]):
            rows.extend(jnp.where(at, part[v], 0.0) for v in range(2))
        lhs_ref[:, s * LANES : (s + 1) * LANES] = jnp.concatenate(rows, axis=0).astype(BF16)
    sums = lax.dot_general(lhs_ref[...], hot_ref[...], NT, preferred_element_type=F32)
    sums = sums[:16] + sums[16:]
    face_catch = sums[:8]
    heat = cool_ref[...] / (1.0 + sums[8:])

    def film_step(film, outflow, run):
        inflow = impact_rate * face_catch + film - outflow + run
        frozen = heat * inflow / (heat + inflow)
        return inflow - frozen, frozen

    film1, frozen1 = film_step(film0, out_ref[0], run0)
    out_ref[1] = film1 * shed

    @pl.when(has_next)
    def _():
        pass_on(1).start()

    @pl.when(has_prev)
    def _():
        await_bytes(prev_ref.at[1], recvs.at[2])

    run1 = runin(prev_ref[1], out_ref[1])
    film2, frozen2 = film_step(film1, out_ref[1], run1)
    film_out[...] = film2
    ice2 = ice_ref[...] + frozen1 + frozen2
    ice_out[...] = ice2

    for g in range(4):
        faces = back_ref[g * 8 : g * 8 + 8, :]
        low, high = faces & 127, faces >> 7
        picked = jnp.zeros((8, LANES), F32)
        for j in range(8):
            value = jnp.take_along_axis(
                jnp.broadcast_to(ice2[j : j + 1], (8, LANES)), low, axis=1,
                mode="promise_in_bounds",
            )
            picked = jnp.where(high == j, value, picked)
        for i in range(4):
            col_ref[0, g * 4 + i] = picked[2 * i : 2 * i + 2]
    to_row(col_ref.at[0], col_ref.at[1], 5)
    col_ref[1, c] = col_ref[0, c]

    wait_normal(1, nr2_ref)

    def second_layer(i):
        x = layer_of(i)

        def emit(t, zs, acc, v0, v1, v2):
            frac_out[x - 1, :, zs] = acc[0]
            for k in range(3):
                mom_out[k, x - 1, :, zs] = acc[1 + k]

        advance(s1_ref, v0_ref, v1_ref, v2_ref, vn_ref, nr2_ref, air_ref, drag_ref, emit, x)

    @pl.loop(0, SECOND_CUT)
    def _(i):
        second_layer(i)

    await_bytes(col_ref.at[1, pl.ds(0, N_SPAN - 1)], recvs.at[5])

    @pl.loop(1, N_NORMAL)
    def _(i):
        there = (n + i) % N_NORMAL
        remote(col_ref.at[1], all_ref.at[n], sends.at[6], recvs.at[6], (c, there)).start()

    all_ref[n] = col_ref[1]

    @pl.loop(SECOND_CUT, NX)
    def _(i):
        @pl.when(i == NX - 2)
        def _():
            for copy in again:
                copy.wait()

        second_layer(i)

    await_bytes(all_ref.at[pl.ds(0, N_NORMAL - 1)], recvs.at[6])

    await_bytes(sendface_ref.at[pl.ds(0, N_SPAN - 1)], sends.at[0])

    @pl.when(has_next)
    def _():
        await_bytes(out_ref.at[0], sends.at[1])
        await_bytes(out_ref.at[1], sends.at[2])

    @pl.when(on_wall)
    def _():
        await_bytes(fw_ref.at[pl.ds(0, OWNERS - N_SPAN)], sends.at[3])

    await_bytes(part_ref.at[pl.ds(0, N_SPAN - 1)], sends.at[4])
    await_bytes(col_ref.at[0, pl.ds(0, N_SPAN - 1)], sends.at[5])
    await_bytes(all_ref.at[pl.ds(0, N_NORMAL - 1)], sends.at[6])


FIRST_CUT = 10
SECOND_CUT = 11


def output_kernel(
    frac_ref, mom_ref, film_ref, ice_ref, all_ref, key8_ref,
    frac_out, mom_out, film_out, ice_out, disp_out,
    pick_ref, row_ref, disp_ref, sems,
):
    n = lax.axis_index("normal")
    put_m = pltpu.make_async_copy(mom_ref, mom_out, sems.at[0])
    put_a = pltpu.make_async_copy(frac_ref, frac_out, sems.at[1])
    put_m.start()
    put_a.start()
    film_out[...] = film_ref[...]
    ice_out[...] = ice_ref[...]

    for h in range(2):
        pick_ref[h * LANES : (h + 1) * LANES, :] = (
            all_ref[:, :, h, :].reshape(OWNERS, LANES).T
        )
    y = (n * NYB + iota((NYB, LANES), 0)).astype(F32) + 0.5
    left = 1.0 - y / (NYB * N_NORMAL)
    profile = left * left
    group = 4
    puts = []
    for g in range(NX // group):

        @pl.loop(g * group, (g + 1) * group)
        def _(x):
            key = key8_ref[x]
            order, rank = key >> 5, key & (SLOTS - 1)
            base = pl.multiple_of((x // 2) * SLOTS, SLOTS)
            table = pick_ref[pl.ds(base, SLOTS), :]
            picked = jnp.zeros((8, LANES), F32)
            for j in range(SLOTS):
                value = jnp.take_along_axis(
                    jnp.broadcast_to(table[j : j + 1], (8, LANES)), order, axis=1,
                    mode="promise_in_bounds",
                )
                picked = jnp.where(rank == j, value, picked)
            row_ref[...] = picked
            for t in range(CH):
                disp_ref[x, :, t * LANES : (t + 1) * LANES] = row_ref[t : t + 1, :] * profile

        part = pl.ds(g * group, group)
        put = pltpu.make_async_copy(disp_ref.at[part], disp_out.at[part], sems.at[2 + g])
        put.start()
        puts.append(put)
    put_m.wait()
    put_a.wait()
    for put in puts:
        put.wait()


def shape(dims, dtype=F32):
    return jax.ShapeDtypeStruct(dims, dtype)


VM = pl.BlockSpec(memory_space=pltpu.VMEM)
HBM = pl.BlockSpec(memory_space=pltpu.HBM)


def per_device(
    volume_fraction, droplet_momentum, air_velocity, drag, wall_owner, wall_face,
    film, ice, cooling, shed, share, upstream,
):
    brick = (NX, NYB, NZ)
    tile = (8, LANES)
    rows = (NX, 1, NZ)
    hbm = functools.partial(pltpu.with_memory_space_constraint, memory_space=pltpu.HBM)
    dma = pltpu.SemaphoreType.DMA
    frac, mom, film_now, ice_now, ice_slots, keys = pl.pallas_call(
        main_kernel,
        out_shape=(
            shape(brick), shape((3,) + brick), shape(tile), shape(tile),
            shape((N_NORMAL, N_SPAN, 2, LANES)), shape((NX, 8, LANES), I32),
        ),
        in_specs=[HBM] * 12,
        out_specs=(VM,) * 6,
        scratch_shapes=[
            pltpu.VMEM(rows, I32),
            pltpu.VMEM((NX, NZ), I32),
            pltpu.VMEM(tile, F32),
            pltpu.VMEM(tile, F32),
            pltpu.VMEM(tile, F32),
            pltpu.VMEM(tile, F32),
            pltpu.VMEM((4, NZ), F32),
            pltpu.VMEM((4, NZ), I32),
            pltpu.VMEM((4, NX + 2, NYB, NZ), F32),
            pltpu.VMEM((4, NX + 2, NYB, NZ), F32),
            pltpu.VMEM((NX + 2, NYB, NZ), F32),
            pltpu.VMEM(brick, F32),
            pltpu.VMEM(brick, F32),
            pltpu.VMEM((2,) + rows, F32),
            pltpu.VMEM((2, 2, 4) + rows, F32),
            pltpu.VMEM((2, 4) + rows, F32),
            pltpu.VMEM((2, 4) + rows, F32),
            pltpu.VMEM((3,) + brick, F32),
            pltpu.VMEM(brick, F32),
            pltpu.VMEM((NX, OWNERS, NZ), BF16),
            pltpu.VMEM(rows, I32),
            pltpu.VMEM((N_SPAN, 2, LANES), I32),
            pltpu.VMEM((14, PR, NZ), F32),
            pltpu.VMEM((7, PR, NZ), F32),
            pltpu.VMEM((3, PR, NZ), F32),
            pltpu.VMEM((2, PR, NZ), F32),
            pltpu.VMEM((2, STRIP, 1, NZ), F32),
            pltpu.VMEM((2, STRIP, 1, NZ), F32),
            pltpu.VMEM((2, 8 * SLOTS, OWNERS), F32),
            pltpu.VMEM((OWNERS, 4, LANES), F32),
            pltpu.VMEM((N_SPAN, 4, LANES), F32),
            pltpu.VMEM((N_SPAN, 4, LANES), F32),
            pltpu.VMEM((N_SPAN, 2, LANES), I32),
            pltpu.VMEM((32, 2 * N_SPAN * LANES), BF16),
            pltpu.VMEM((LANES, 2 * N_SPAN * LANES), BF16),
            pltpu.VMEM((4, 8, LANES), I32),
            pltpu.VMEM((4, 8, LANES), F32),
            pltpu.VMEM((2, 8, LANES), F32),
            pltpu.VMEM((2, 8, LANES), F32),
            pltpu.VMEM((2 * N_SPAN, LANES), I32),
            pltpu.VMEM((2, N_SPAN, 2, LANES), F32),
            dma((4,)), dma((8,)), dma((4,)), dma((4,)), dma((4,)), dma((4,)), dma((2,)), dma((2,)),
            dma((7,)), dma((7,)),
        ],
        compiler_params=pltpu.CompilerParams(
            collective_id=0, has_side_effects=True, vmem_limit_bytes=40 * MB
        ),
        name="accretion",
    )(
        *map(
            hbm,
            (
                volume_fraction, droplet_momentum, air_velocity, drag,
                wall_owner.reshape(rows), wall_face,
                film.reshape(tile), ice.reshape(tile), cooling.reshape(tile), shed.reshape(tile),
                share, upstream,
            ),
        )
    )

    fraction_out, momentum_out, film_out, ice_out, displacement = pl.pallas_call(
        output_kernel,
        out_shape=(
            shape(brick), shape((3,) + brick), shape(tile), shape(tile), shape(brick),
        ),
        in_specs=[VM] * 6,
        out_specs=(HBM, HBM, VM, VM, HBM),
        scratch_shapes=[
            pltpu.VMEM((8 * SLOTS, OWNERS), F32),
            pltpu.VMEM((8, LANES), F32),
            pltpu.VMEM(brick, F32),
            dma((6,)),
        ],
        compiler_params=pltpu.CompilerParams(vmem_limit_bytes=32 * MB),
        name="results",
    )(frac, mom, film_now, ice_now, ice_slots, keys)
    return fraction_out, momentum_out, film_out.reshape(-1), ice_out.reshape(-1), displacement


def solution(mesh):
    volume = P("span", "normal", None)
    vector = P(None, "span", "normal", None)
    faces = P(("span", "normal"))
    links = P(None, ("span", "normal"))
    return jax.shard_map(
        per_device,
        mesh=mesh,
        in_specs=(
            volume, vector, vector, volume, P("span", None, None), P("span", None),
            faces, faces, faces, faces, links, links,
        ),
        out_specs=(volume, vector, faces, faces, volume),
        check_vma=False,
    )
```

time: 84.4 us -> 44.9 us (0.53)
  Pallas kernels: 78.6 us -> 44.1 us
  local copies, waits for them, and re-layouts: 4.29 us -> 0 us
    pallas_call x5 -> x2, Pallas kernels: 78.6 us -> 44.1 us  [the longest x1 40.7 us: per_device(): pl.pallas_call(main_kernel, out_shape=(shape(brick), shape((3,) + brick),...]
    unnamed x24 -> x0, local copies, waits for them, and re-layouts: 4.29 us -> none
where the time goes in v1:
time: 44.9 us; the launch traced here: 44.7 us
  Pallas kernels  44.1 us (98%)
  between operations  0.64 us (1%)
    pallas_call x1, Pallas kernels, per_device(): pl.pallas_call(main_kernel, out_shape=(shape(brick), shape((3,) + brick),...  40.7 us
    pallas_call x1, Pallas kernels, per_device(): pl.pallas_call(output_kernel, out_shape=(shape(brick), shape((3,) + brick...  3.36 us

profile of v1, /device:TPU:1, one launch (start us, length us, event | category | flops | bytes accessed | tf_op | source)
XLA Modules:
  0.0 44.7 jit_solution(12989655279747469986)
XLA Ops:
  0.6 40.7 %accretion.1 = (f32[16,16,1024]{2,1,0:T(8,128)S(1)}, f32[3,16,16,1024]{3,2,1,0:T(8,128)S(1)}, f32[8,128]{1,0:T(8,128)S(1)}, f32[8,128]{1,0:T(8,128)S(1)}, f32[8,...) custom-call(f32[16,16,1024]{2,1,0:T(8,128)} %a_hbm.1, f32[3,16,16,1024]{3,2,1,0:T(8,128)} %m_hbm.1, ...), custom_call_target="tpu_custom_call" | custom-call | tf_op jit(solution)/shard_map/accretion/pallas_call | solution.py:776
  41.4 3.4 %results.1 = (f32[16,16,1024]{2,1,0:T(8,128)}, f32[3,16,16,1024]{3,2,1,0:T(8,128)}, f32[8,128]{1,0:T(8,128)}, f32[8,128]{1,0:T(8,128)}, f32[16,16,1024]{2,1,0:T(8,128)}) custom-call(f32[16,16,1024]{2,1,0:T(8,128)S(1)} %get-tuple-element.16.frac_ref, f32[3,16,16,1024]{3,2,1,0:T(8,128)S(1)} %get-tuple-element.17.mom_ref, ...), custom_call_target="tpu_custom_call" | custom-call | tf_op jit(solution)/shard_map/results/pallas_call | solution.py:845

commit v2 on v1

--- a/solution.py
+++ b/solution.py
@@ -108,53 +108,51 @@
     return jnp.where(i < NX - 2, i + 2, jnp.where(i == NX - 2, 1, NX))
 
 
-def prepare(owner_ref, face_ref, rank_ref, key8_ref, send_ref, hot_ref, n):
+def prepare(owner_ref, face_ref, rank_ref, key8_ref, send_ref, hot_ref, n, h):
     q_len = 256
     quarters = NZ // q_len
     tri = (iota((q_len, q_len), 0) <= iota((q_len, q_len), 1)).astype(F32).astype(BF16)
     names = iota((OWNERS, q_len), 0)
     mine = n * N_SPAN + iota((N_SPAN, NZ), 0)
     slot = iota((SLOTS, NZ), 0)
-    for h in range(2):
-        pieces = []
-        for b in range(4):
-            offset = jnp.zeros((OWNERS, 1), F32)
-            got = jnp.zeros((N_SPAN, 2 * SLOTS), F32)
-            for half in range(2):
-                x = h * 8 + b * 2 + half
-                owner = owner_ref[x]
-                order = (owner & (N_NORMAL - 1)) * N_SPAN + (owner >> 3)
-                hots = []
-                for q in range(quarters):
-                    qs = slice(q * q_len, (q + 1) * q_len)
-                    hot = (order[:, qs] == names).astype(F32).astype(BF16)
-                    hot_ref[x, :, qs] = hot
-                    hots.append(hot)
-                counts = jnp.dot(
-                    jnp.concatenate(hots, axis=0), tri, preferred_element_type=F32
+    pieces = []
+    for b in range(4):
+        offset = jnp.zeros((OWNERS, 1), F32)
+        got = jnp.zeros((N_SPAN, 2 * SLOTS), F32)
+        for half in range(2):
+            x = h * 8 + b * 2 + half
+            owner = owner_ref[x]
+            order = (owner & (N_NORMAL - 1)) * N_SPAN + (owner >> 3)
+            hots = []
+            for q in range(quarters):
+                qs = slice(q * q_len, (q + 1) * q_len)
+                hot = (order[:, qs] == names).astype(F32).astype(BF16)
+                hot_ref[x, :, qs] = hot
+                hots.append(hot)
+            counts = jnp.dot(
+                jnp.concatenate(hots, axis=0), tri, preferred_element_type=F32
+            )
+            ranks = []
+            for q in range(quarters):
+                part = counts[q * OWNERS : (q + 1) * OWNERS]
+                ranks.append(
+                    jnp.sum(hots[q].astype(F32) * (part + offset), axis=0, keepdims=True) - 1.0
                 )
-                ranks = []
-                for q in range(quarters):
-                    hot = order[:, q * q_len : (q + 1) * q_len] == names
-                    part = counts[q * OWNERS : (q + 1) * OWNERS]
-                    ranks.append(
-                        jnp.sum(jnp.where(hot, part + offset, 0.0), axis=0, keepdims=True) - 1.0
-                    )
-                    offset = offset + part[:, q_len - 1 : q_len]
-                rank = jnp.concatenate(ranks, axis=1).astype(I32)
-                rank_ref[x] = rank
-                key = order * SLOTS + rank
-                for t in range(CH):
-                    key8_ref[x, t : t + 1, :] = key[:, t * LANES : (t + 1) * LANES]
-                face = face_ref[x : x + 1, :]
-                at = slot == rank
-                high = jnp.where(at, (face >> 7).astype(F32), 0.0)
-                low = jnp.where(at, (face & 127).astype(F32), 0.0)
-                placed = jnp.concatenate([high, low], axis=0).astype(BF16)
-                hot16 = (order == mine).astype(F32).astype(BF16)
-                got = got + lax.dot_general(hot16, placed, NT, preferred_element_type=F32)
-            pieces.append(got[:, :SLOTS] * 128.0 + got[:, SLOTS:])
-        send_ref[:, h, :] = jnp.concatenate(pieces, axis=1).astype(I32)
+                offset = offset + part[:, q_len - 1 : q_len]
+            rank = jnp.concatenate(ranks, axis=1).astype(I32)
+            rank_ref[x] = rank
+            key = order * SLOTS + rank
+            for t in range(CH):
+                key8_ref[x, t : t + 1, :] = key[:, t * LANES : (t + 1) * LANES]
+            face = face_ref[x : x + 1, :]
+            at = slot == rank
+            high = jnp.where(at, (face >> 7).astype(F32), 0.0)
+            low = jnp.where(at, (face & 127).astype(F32), 0.0)
+            placed = jnp.concatenate([high, low], axis=0).astype(BF16)
+            hot16 = (order == mine).astype(F32).astype(BF16)
+            got = got + lax.dot_general(hot16, placed, NT, preferred_element_type=F32)
+        pieces.append(got[:, :SLOTS] * 128.0 + got[:, SLOTS:])
+    send_ref[:, h, :] = jnp.concatenate(pieces, axis=1).astype(I32)
 
 
 PR = 24
@@ -278,11 +276,31 @@
         pltpu.make_async_copy(src, dst, small_sem.at[i])
         for i, (src, dst) in enumerate(((owner_hbm, owner_ref), (face_hbm, face_ref)))
     ]
+    low, high = pl.ds(0, 8), pl.ds(8, 8)
+    whole = pl.ds(1, NX)
+    low_loads = [
+        pltpu.make_async_copy(src, dst, load_sem.at[i])
+        for i, (src, dst) in enumerate(
+            (
+                (a_hbm.at[:, low], s_ref.at[0, whole, low]),
+                (m_hbm.at[:, :, low], s_ref.at[pl.ds(1, 3), whole, low]),
+                (air_hbm.at[1, :, low], air_ref.at[1, :, low]),
+                (drag_hbm.at[:, low], drag_ref.at[:, low]),
+            )
+        )
+    ]
     loads = [
-        pltpu.make_async_copy(a_hbm, s_ref.at[0, pl.ds(1, NX)], load_sem.at[0]),
-        pltpu.make_async_copy(m_hbm, s_ref.at[pl.ds(1, 3), pl.ds(1, NX)], load_sem.at[1]),
-        pltpu.make_async_copy(air_hbm, air_ref, load_sem.at[2]),
-        pltpu.make_async_copy(drag_hbm, drag_ref, load_sem.at[3]),
+        pltpu.make_async_copy(src, dst, load_sem.at[4 + i])
+        for i, (src, dst) in enumerate(
+            (
+                (a_hbm.at[:, high], s_ref.at[0, whole, high]),
+                (m_hbm.at[:, :, high], s_ref.at[pl.ds(1, 3), whole, high]),
+                (air_hbm.at[1, :, high], air_ref.at[1, :, high]),
+                (drag_hbm.at[:, high], drag_ref.at[:, high]),
+                (air_hbm.at[0], air_ref.at[0]),
+                (air_hbm.at[2], air_ref.at[2]),
+            )
+        )
     ] + [
         pltpu.make_async_copy(src, dst, small_sem.at[2 + i])
         for i, (src, dst) in enumerate(
@@ -290,7 +308,7 @@
              (share_hbm, share_ref), (up_hbm, up_ref))
         )
     ]
-    for load in first_loads + loads:
+    for load in first_loads + low_loads + loads:
         load.start()
 
     barrier = pltpu.get_barrier_semaphore()
@@ -313,40 +331,28 @@
 
     for load in first_loads:
         load.wait()
-    prepare(owner_ref, face_ref, rank_ref, key8_ref, sendface_ref, owner_hot, n)
-    for load in loads:
+    prepare(owner_ref, face_ref, rank_ref, key8_ref, sendface_ref, owner_hot, n, 0)
+    for load in low_loads:
         load.wait()
 
+    def packed_row(i, x):
+        if i in FR:
+            return s_ref[0, x + 1, FR.index(i) : FR.index(i) + 1, :]
+        for k, sets in ((1, MS), (2, MN), (3, MC)):
+            if i in sets:
+                y = sets.index(i)
+                return s_ref[k, x + 1, y : y + 1, :]
+        if i in AN:
+            return air_ref[1, x, AN.index(i) : AN.index(i) + 1, :]
+        return drag_ref[x, DR.index(i) : DR.index(i) + 1, :]
+
     @pl.when(on_wall)
     def _():
-        for i in range(14):
-            pk[i, 0:8, :] = jnp.ones((8, NZ), F32)
-            pk[i, 16:24, :] = jnp.ones((8, NZ), F32)
-        for x in range(NX):
-            at = slice(x + 2, x + 3)
-            for y in range(3):
-                pk[FR[y], at, :] = s_ref[0, x + 1, y : y + 1, :]
-                pk[MN[y], at, :] = s_ref[2, x + 1, y : y + 1, :]
-                if y < 2:
-                    pk[MS[y], at, :] = s_ref[1, x + 1, y : y + 1, :]
-                    pk[MC[y], at, :] = s_ref[3, x + 1, y : y + 1, :]
-                    pk[AN[y], at, :] = air_ref[1, x, y : y + 1, :]
-                    pk[DR[y], at, :] = drag_ref[x, y : y + 1, :]
         for side, near, far in ((0, NX - 1, NX - 2), (1, 0, 1)):
             for j, i in enumerate(NEAR):
-                strip_out[side, j] = pk[i, near + 2 : near + 3, :]
+                strip_out[side, j] = packed_row(i, near)
             for j, i in enumerate(FAR):
-                strip_out[side, len(NEAR) + j] = pk[i, far + 2 : far + 3, :]
-
-    @pl.loop(0, NX)
-    def _(x):
-        for k in range(4):
-            ns_ref[0, 0, k, x] = s_ref[k, x + 1, 0:1, :]
-            ns_ref[0, 1, k, x] = s_ref[k, x + 1, NYB - 1 : NYB, :]
-
-    film0 = film_ref[...]
-    shed = shed_ref[...]
-    out_ref[0] = film0 * shed
+                strip_out[side, len(NEAR) + j] = packed_row(i, far)
 
     @pl.when(jnp.logical_not(has_prev))
     def _():
@@ -372,10 +378,16 @@
     def await_bytes(ref, sem):
         pltpu.make_async_copy(ref, ref, sem).wait()
 
+    def far_first(place, i):
+        return (place + jnp.where(i == 3, 0, jnp.where(i == 0, 2, 2 * i - 1))) & 3
+
+    def row_peer(i):
+        return far_first(c >> 2, i >> 2) * 4 + far_first(c & 3, i & 3)
+
     def to_row(src, dst, which):
-        @pl.loop(1, N_SPAN)
+        @pl.loop(0, N_SPAN - 1)
         def _(i):
-            there = (c + i) % N_SPAN
+            there = row_peer(i)
             remote(src.at[there], dst.at[c], sends.at[which], recvs.at[which], (there, n)).start()
 
     strips = [
@@ -438,9 +450,22 @@
             for i, (there, layer, target) in enumerate(((right, NX, 0), (left, 1, NX + 1)))
         ]
 
+    for load in loads:
+        load.wait()
+
+    @pl.loop(0, NX)
+    def _(x):
+        for k in range(4):
+            ns_ref[0, 0, k, x] = s_ref[k, x + 1, 0:1, :]
+            ns_ref[0, 1, k, x] = s_ref[k, x + 1, NYB - 1 : NYB, :]
+
     start_normal(0, nr_ref)
-    to_row(sendface_ref, gotface_ref, 0)
-    gotface_ref[c] = sendface_ref[c]
+    spans = span_copies(s_ref, s_ref, 0)
+    for copy in spans:
+        copy.start()
+    film0 = film_ref[...]
+    shed = shed_ref[...]
+    out_ref[0] = film0 * shed
 
     def pass_on(step):
         return remote(out_ref.at[step], prev_ref.at[step], sends.at[1 + step],
@@ -450,12 +475,25 @@
     def _():
         pass_on(0).start()
 
-    spans = span_copies(s_ref, s_ref, 0)
-    for copy in spans:
-        copy.start()
+    prepare(owner_ref, face_ref, rank_ref, key8_ref, sendface_ref, owner_hot, n, 1)
+    to_row(sendface_ref, gotface_ref, 0)
+    gotface_ref[c] = sendface_ref[c]
+
+    @pl.loop(0, NX)
+    def _(x):
+        scale = half_step / s_ref[0, x + 1]
+        v0_ref[x + 1] = s_ref[1, x + 1] * scale
+        v1_ref[x] = s_ref[2, x + 1] * scale
+        v2_ref[x] = s_ref[3, x + 1] * scale
 
     @pl.when(on_wall)
     def _():
+        for i in range(14):
+            pk[i, 0:8, :] = jnp.ones((8, NZ), F32)
+            pk[i, 16:24, :] = jnp.ones((8, NZ), F32)
+        for x in range(NX):
+            for i in range(14):
+                pk[i, x + 2 : x + 3, :] = packed_row(i, x)
         for copy in strips:
             copy.wait()
         for side, near, far in ((0, 1, 0), (1, NX + 2, NX + 3)):
@@ -466,7 +504,7 @@
         wall_strip(pk, vq, q1, wv)
         slot = iota((SLOTS, NZ), 0)
 
-        @pl.loop(0, NX // 2)
+        @pl.loop(0, NX // 2, unroll=2)
         def _(b):
             total = jnp.zeros((4 * SLOTS, OWNERS), F32)
             for half in range(2):
@@ -491,20 +529,14 @@
             for h in range(2):
                 fw_ref[:, 2 * v + h, :] = slots_ref[v, h * LANES : (h + 1) * LANES, :].T
 
-        @pl.loop(1, N_NORMAL)
+        @pl.loop(0, N_NORMAL - 1)
         def _(i):
-            remote(fw_ref.at[pl.ds(i * N_SPAN, N_SPAN)], part_ref, sends.at[3], recvs.at[3],
-                   (c, i)).start()
+            there = 2 * far_first(0, i >> 1) + 1 - (i & 1)
+            remote(fw_ref.at[pl.ds(there * N_SPAN, N_SPAN)], part_ref, sends.at[3], recvs.at[3],
+                   (c, there)).start()
 
         part_ref[...] = fw_ref[0:N_SPAN]
         to_row(part_ref, got_ref, 4)
-
-    @pl.loop(0, NX)
-    def _(x):
-        scale = half_step / s_ref[0, x + 1]
-        v0_ref[x + 1] = s_ref[1, x + 1] * scale
-        v1_ref[x] = s_ref[2, x + 1] * scale
-        v2_ref[x] = s_ref[3, x + 1] * scale
 
     for k in range(4):
         for t in range(8):
@@ -645,9 +677,16 @@
             )
             picked = jnp.where(high == j, value, picked)
         for i in range(4):
-            col_ref[0, g * 4 + i] = picked[2 * i : 2 * i + 2]
-    to_row(col_ref.at[0], col_ref.at[1], 5)
-    col_ref[1, c] = col_ref[0, c]
+            col_ref[g * 4 + i] = picked[2 * i : 2 * i + 2]
+
+    @pl.loop(0, OWNERS - 1)
+    def _(i):
+        there = row_peer(i >> 3)
+        side = 2 * far_first(n >> 1, (i >> 1) & 3) + ((n + 1 + i) & 1)
+        remote(col_ref.at[there], all_ref.at[n * N_SPAN + c], sends.at[5], recvs.at[5],
+               (there, side)).start()
+
+    all_ref[n * N_SPAN + c] = col_ref[c]
 
     wait_normal(1, nr2_ref)
 
@@ -661,20 +700,7 @@
 
         advance(s1_ref, v0_ref, v1_ref, v2_ref, vn_ref, nr2_ref, air_ref, drag_ref, emit, x)
 
-    @pl.loop(0, SECOND_CUT)
-    def _(i):
-        second_layer(i)
-
-    await_bytes(col_ref.at[1, pl.ds(0, N_SPAN - 1)], recvs.at[5])
-
-    @pl.loop(1, N_NORMAL)
-    def _(i):
-        there = (n + i) % N_NORMAL
-        remote(col_ref.at[1], all_ref.at[n], sends.at[6], recvs.at[6], (c, there)).start()
-
-    all_ref[n] = col_ref[1]
-
-    @pl.loop(SECOND_CUT, NX)
+    @pl.loop(0, NX)
     def _(i):
         @pl.when(i == NX - 2)
         def _():
@@ -683,7 +709,7 @@
 
         second_layer(i)
 
-    await_bytes(all_ref.at[pl.ds(0, N_NORMAL - 1)], recvs.at[6])
+    await_bytes(all_ref.at[pl.ds(0, OWNERS - 1)], recvs.at[5])
 
     await_bytes(sendface_ref.at[pl.ds(0, N_SPAN - 1)], sends.at[0])
 
@@ -697,12 +723,10 @@
         await_bytes(fw_ref.at[pl.ds(0, OWNERS - N_SPAN)], sends.at[3])
 
     await_bytes(part_ref.at[pl.ds(0, N_SPAN - 1)], sends.at[4])
-    await_bytes(col_ref.at[0, pl.ds(0, N_SPAN - 1)], sends.at[5])
-    await_bytes(all_ref.at[pl.ds(0, N_NORMAL - 1)], sends.at[6])
+    await_bytes(all_ref.at[pl.ds(0, OWNERS - 1)], sends.at[5])
 
 
 FIRST_CUT = 10
-SECOND_CUT = 11
 
 
 def output_kernel(
@@ -715,12 +739,14 @@
     put_a = pltpu.make_async_copy(frac_ref, frac_out, sems.at[1])
     put_m.start()
     put_a.start()
-    film_out[...] = film_ref[...]
-    ice_out[...] = ice_ref[...]
+    put_film = pltpu.make_async_copy(film_ref, film_out, sems.at[6])
+    put_ice = pltpu.make_async_copy(ice_ref, ice_out, sems.at[7])
+    put_film.start()
+    put_ice.start()
 
     for h in range(2):
         pick_ref[h * LANES : (h + 1) * LANES, :] = (
-            all_ref[:, :, h, :].reshape(OWNERS, LANES).T
+            all_ref[:, h, :].T
         )
     y = (n * NYB + iota((NYB, LANES), 0)).astype(F32) + 0.5
     left = 1.0 - y / (NYB * N_NORMAL)
@@ -750,8 +776,8 @@
         put = pltpu.make_async_copy(disp_ref.at[part], disp_out.at[part], sems.at[2 + g])
         put.start()
         puts.append(put)
-    put_m.wait()
-    put_a.wait()
+    for put in (put_m, put_a, put_film, put_ice):
+        put.wait()
     for put in puts:
         put.wait()
 
@@ -777,7 +803,7 @@
         main_kernel,
         out_shape=(
             shape(brick), shape((3,) + brick), shape(tile), shape(tile),
-            shape((N_NORMAL, N_SPAN, 2, LANES)), shape((NX, 8, LANES), I32),
+            shape((OWNERS, 2, LANES)), shape((NX, 8, LANES), I32),
         ),
         in_specs=[HBM] * 12,
         out_specs=(VM,) * 6,
@@ -822,9 +848,9 @@
             pltpu.VMEM((2, 8, LANES), F32),
             pltpu.VMEM((2, 8, LANES), F32),
             pltpu.VMEM((2 * N_SPAN, LANES), I32),
-            pltpu.VMEM((2, N_SPAN, 2, LANES), F32),
-            dma((4,)), dma((8,)), dma((4,)), dma((4,)), dma((4,)), dma((4,)), dma((2,)), dma((2,)),
-            dma((7,)), dma((7,)),
+            pltpu.VMEM((N_SPAN, 2, LANES), F32),
+            dma((10,)), dma((8,)), dma((4,)), dma((4,)), dma((4,)), dma((4,)), dma((2,)), dma((2,)),
+            dma((6,)), dma((6,)),
         ],
         compiler_params=pltpu.CompilerParams(
             collective_id=0, has_side_effects=True, vmem_limit_bytes=40 * MB
@@ -848,12 +874,12 @@
             shape(brick), shape((3,) + brick), shape(tile), shape(tile), shape(brick),
         ),
         in_specs=[VM] * 6,
-        out_specs=(HBM, HBM, VM, VM, HBM),
+        out_specs=(HBM,) * 5,
         scratch_shapes=[
             pltpu.VMEM((8 * SLOTS, OWNERS), F32),
             pltpu.VMEM((8, LANES), F32),
             pltpu.VMEM(brick, F32),
-            dma((6,)),
+            dma((8,)),
         ],
         compiler_params=pltpu.CompilerParams(vmem_limit_bytes=32 * MB),
         name="results",

time: 44.9 us -> 41.8 us (0.931)
  Pallas kernels: 44.1 us -> 40.8 us
    pallas_call x1, Pallas kernels: 40.7 us -> 38 us  [per_device(): pl.pallas_call(main_kernel, out_shape=(shape(brick), shape((3,) + brick),...]
    pallas_call x1, Pallas kernels: 3.36 us -> 2.78 us  [per_device(): pl.pallas_call(output_kernel, out_shape=(shape(brick), shape((3,) + brick...]
where the time goes in v2:
time: 41.8 us; the launch traced here: 41.4 us
  Pallas kernels  40.8 us (98%)
  between operations  0.64 us (2%)
    pallas_call x1, Pallas kernels, per_device(): pl.pallas_call(main_kernel, out_shape=(shape(brick), shape((3,) + brick),...  38 us
    pallas_call x1, Pallas kernels, per_device(): pl.pallas_call(output_kernel, out_shape=(shape(brick), shape((3,) + brick...  2.78 us

profile of v2, /device:TPU:1, one launch (start us, length us, event | category | flops | bytes accessed | tf_op | source)
XLA Modules:
  0.0 41.4 jit_solution(6319344187353108393)
XLA Ops:
  0.6 38.0 %accretion.1 = (f32[16,16,1024]{2,1,0:T(8,128)S(1)}, f32[3,16,16,1024]{3,2,1,0:T(8,128)S(1)}, f32[8,128]{1,0:T(8,128)S(1)}, f32[8,128]{1,0:T(8,128)S(1)}, f32[12...) custom-call(f32[16,16,1024]{2,1,0:T(8,128)} %a_hbm.1, f32[3,16,16,1024]{3,2,1,0:T(8,128)} %m_hbm.1, ...), custom_call_target="tpu_custom_call" | custom-call | tf_op jit(solution)/shard_map/accretion/pallas_call | solution.py:802
  38.6 2.8 %results.1 = (f32[16,16,1024]{2,1,0:T(8,128)}, f32[3,16,16,1024]{3,2,1,0:T(8,128)}, f32[8,128]{1,0:T(8,128)}, f32[8,128]{1,0:T(8,128)}, f32[16,16,1024]{2,1,0:T(8,128)}) custom-call(f32[16,16,1024]{2,1,0:T(8,128)S(1)} %get-tuple-element.16.frac_ref, f32[3,16,16,1024]{3,2,1,0:T(8,128)S(1)} %get-tuple-element.17.mom_ref, ...), custom_call_target="tpu_custom_call" | custom-call | tf_op jit(solution)/shard_map/results/pallas_call | solution.py:871

commit v3 on v2

--- a/solution.py
+++ b/solution.py
@@ -104,16 +104,12 @@
     )
 
 
-def layer_of(i):
-    return jnp.where(i < NX - 2, i + 2, jnp.where(i == NX - 2, 1, NX))
-
-
 def prepare(owner_ref, face_ref, rank_ref, key8_ref, send_ref, hot_ref, n, h):
     q_len = 256
     quarters = NZ // q_len
     tri = (iota((q_len, q_len), 0) <= iota((q_len, q_len), 1)).astype(F32).astype(BF16)
     names = iota((OWNERS, q_len), 0)
-    mine = n * N_SPAN + iota((N_SPAN, NZ), 0)
+    mine = N_NORMAL * iota((N_SPAN, NZ), 0) + n
     slot = iota((SLOTS, NZ), 0)
     pieces = []
     for b in range(4):
@@ -122,11 +118,10 @@
         for half in range(2):
             x = h * 8 + b * 2 + half
             owner = owner_ref[x]
-            order = (owner & (N_NORMAL - 1)) * N_SPAN + (owner >> 3)
             hots = []
             for q in range(quarters):
                 qs = slice(q * q_len, (q + 1) * q_len)
-                hot = (order[:, qs] == names).astype(F32).astype(BF16)
+                hot = (owner[:, qs] == names).astype(F32).astype(BF16)
                 hot_ref[x, :, qs] = hot
                 hots.append(hot)
             counts = jnp.dot(
@@ -141,7 +136,7 @@
                 offset = offset + part[:, q_len - 1 : q_len]
             rank = jnp.concatenate(ranks, axis=1).astype(I32)
             rank_ref[x] = rank
-            key = order * SLOTS + rank
+            key = owner * SLOTS + rank
             for t in range(CH):
                 key8_ref[x, t : t + 1, :] = key[:, t * LANES : (t + 1) * LANES]
             face = face_ref[x : x + 1, :]
@@ -149,7 +144,7 @@
             high = jnp.where(at, (face >> 7).astype(F32), 0.0)
             low = jnp.where(at, (face & 127).astype(F32), 0.0)
             placed = jnp.concatenate([high, low], axis=0).astype(BF16)
-            hot16 = (order == mine).astype(F32).astype(BF16)
+            hot16 = (owner == mine).astype(F32).astype(BF16)
             got = got + lax.dot_general(hot16, placed, NT, preferred_element_type=F32)
         pieces.append(got[:, :SLOTS] * 128.0 + got[:, SLOTS:])
     send_ref[:, h, :] = jnp.concatenate(pieces, axis=1).astype(I32)
@@ -256,9 +251,9 @@
     owner_ref, face_ref, film_ref, ice_ref, cool_ref, shed_ref, share_ref, up_ref,
     s_ref, s1_ref, v0_ref, v1_ref, v2_ref, vn_ref, ns_ref, nr_ref, nr2_ref, air_ref, drag_ref,
     owner_hot, rank_ref, sendface_ref, pk, vq, q1, wv, strip_out, strip_in,
-    slots_ref, fw_ref, part_ref, got_ref, gotface_ref, lhs_ref, hot_ref,
-    links_ref, weight_ref, prev_ref, out_ref, back_ref, col_ref,
-    load_sem, small_sem, span_send, span_recv, normal_send, normal_recv, strip_send, strip_recv, sends, recvs,
+    slots_ref, fw_ref, got_ref, gotface_ref, prevface_ref, lhs_ref, hot_ref, gone_ref,
+    links_ref, weight_ref, prev_ref, out_ref, pack_ref, prevpack_ref, back_ref, col_ref,
+    load_sem, small_sem, span_send, span_recv, normal_send, normal_recv, strip_send, strip_recv, sends, recvs, ready,
 ):
     c, n = lax.axis_index("span"), lax.axis_index("normal")
     right, left = (c + 1) % N_SPAN, (c + N_SPAN - 1) % N_SPAN
@@ -356,7 +351,9 @@
 
     @pl.when(jnp.logical_not(has_prev))
     def _():
-        prev_ref[...] = jnp.zeros((2, 8, LANES), F32)
+        prev_ref[...] = jnp.zeros((8, LANES), F32)
+        prevpack_ref[...] = jnp.ones((4, 8, LANES), F32)
+        prevface_ref[...] = jnp.zeros((N_SPAN, 2, LANES), I32)
 
     crossing = jnp.logical_or(cross_next, cross_prev)
     peers = N_SPAN + N_NORMAL - 2
@@ -383,6 +380,20 @@
 
     def row_peer(i):
         return far_first(c >> 2, i >> 2) * 4 + far_first(c & 3, i & 3)
+
+    sides = [2 * ((n >> 1) + j & 3) + core for j in (2, 1, 3, 0) for core in range(2)]
+    here_last = [2 * ((n >> 1) + j & 3) + core for j in (2, 1, 3) for core in range(2)] + [n ^ 1]
+
+    def to_all(src, dst, which):
+        @pl.loop(0, N_SPAN - 1)
+        def _(i):
+            there = row_peer(i)
+            for side in sides:
+                remote(src(there, side), dst, sends.at[which], recvs.at[which],
+                       (there, side)).start()
+
+        for side in here_last:
+            remote(src(c, side), dst, sends.at[which], recvs.at[which], (c, side)).start()
 
     def to_row(src, dst, which):
         @pl.loop(0, N_SPAN - 1)
@@ -403,16 +414,21 @@
         for copy in strips:
             copy.start()
 
-    def normal_copies(base, dst):
+        @pl.loop(1, N_SPAN)
+        def _(i):
+            pl.semaphore_signal(ready, 1, device_id=((c + i) % N_SPAN, n), device_id_type=MESH)
+
+    def normal_copies(base, dst, sem, start, size):
+        part = pl.ds(start, size)
         return (
-            remote(ns_ref.at[base, 0], dst.at[1], normal_send.at[2 * base],
-                   normal_recv.at[2 * base], (c, n - 1)),
-            remote(ns_ref.at[base, 1], dst.at[0], normal_send.at[2 * base + 1],
-                   normal_recv.at[2 * base + 1], (c, n + 1)),
-        )
-
-    def start_normal(base, dst):
-        low, high = normal_copies(base, dst)
+            remote(ns_ref.at[base, 0, :, part], dst.at[1, :, part], normal_send.at[2 * sem],
+                   normal_recv.at[2 * sem], (c, n - 1)),
+            remote(ns_ref.at[base, 1, :, part], dst.at[0, :, part], normal_send.at[2 * sem + 1],
+                   normal_recv.at[2 * sem + 1], (c, n + 1)),
+        )
+
+    def start_normal(*which):
+        low, high = normal_copies(*which)
 
         @pl.when(has_low)
         def _():
@@ -422,8 +438,8 @@
         def _():
             high.start()
 
-    def wait_normal(base, dst):
-        low, high = normal_copies(base, dst)
+    def wait_normal(*which):
+        low, high = normal_copies(*which)
 
         @pl.when(has_low)
         def _():
@@ -435,6 +451,7 @@
             high.wait_send()
             low.wait_recv()
 
+    def close_edges(dst):
         @pl.when(jnp.logical_not(has_low))
         def _():
             dst[0] = jnp.zeros(dst.shape[1:], F32)
@@ -459,21 +476,27 @@
             ns_ref[0, 0, k, x] = s_ref[k, x + 1, 0:1, :]
             ns_ref[0, 1, k, x] = s_ref[k, x + 1, NYB - 1 : NYB, :]
 
-    start_normal(0, nr_ref)
+    first_halo = (0, nr_ref, 0, 0, NX)
+    again_halo = [
+        (1, nr2_ref, 1 + i, start, size) for i, (start, size) in enumerate(((1, 8), (9, 7), (0, 1)))
+    ]
+    start_normal(*first_halo)
+    close_edges(nr_ref)
+    close_edges(nr2_ref)
     spans = span_copies(s_ref, s_ref, 0)
     for copy in spans:
         copy.start()
     film0 = film_ref[...]
     shed = shed_ref[...]
-    out_ref[0] = film0 * shed
-
-    def pass_on(step):
-        return remote(out_ref.at[step], prev_ref.at[step], sends.at[1 + step],
-                      recvs.at[1 + step], (next_c, next_n))
+    outflow0 = film0 * shed
+    out_ref[...] = outflow0
+
+    def pass_on(src, dst, which):
+        return remote(src, dst, sends.at[which], recvs.at[which], (next_c, next_n))
 
     @pl.when(has_next)
     def _():
-        pass_on(0).start()
+        pass_on(out_ref, prev_ref, 1).start()
 
     prepare(owner_ref, face_ref, rank_ref, key8_ref, sendface_ref, owner_hot, n, 1)
     to_row(sendface_ref, gotface_ref, 0)
@@ -525,18 +548,16 @@
             slots_ref[0, spot, :] = both[:SLOTS]
             slots_ref[1, spot, :] = both[SLOTS:]
 
+        fw_ref[0] = jnp.zeros((4, LANES), F32)
         for v in range(2):
             for h in range(2):
-                fw_ref[:, 2 * v + h, :] = slots_ref[v, h * LANES : (h + 1) * LANES, :].T
-
-        @pl.loop(0, N_NORMAL - 1)
-        def _(i):
-            there = 2 * far_first(0, i >> 1) + 1 - (i & 1)
-            remote(fw_ref.at[pl.ds(there * N_SPAN, N_SPAN)], part_ref, sends.at[3], recvs.at[3],
-                   (c, there)).start()
-
-        part_ref[...] = fw_ref[0:N_SPAN]
-        to_row(part_ref, got_ref, 4)
+                fw_ref[1:, 2 * v + h, :] = slots_ref[v, h * LANES : (h + 1) * LANES, :].T
+        pl.semaphore_wait(ready, N_SPAN - 1)
+
+        to_all(
+            lambda there, side: fw_ref.at[pl.ds(there * N_NORMAL + side, 2)], got_ref.at[c], 3
+        )
+        got_ref[c] = fw_ref[pl.ds(c * N_NORMAL, 2)]
 
     for k in range(4):
         for t in range(8):
@@ -544,16 +565,24 @@
             weight_ref[k, t : t + 1, :] = share_ref[k : k + 1, t * LANES : (t + 1) * LANES]
     await_bytes(gotface_ref.at[pl.ds(0, N_SPAN - 1)], recvs.at[0])
     lanes_high = iota((LANES, LANES), 0)
-    for s in range(2 * N_SPAN):
-        face = gotface_ref[s // 2][s % 2 : s % 2 + 1]
-        hot_ref[:, s * LANES : (s + 1) * LANES] = (
-            (lanes_high == (face & 127)).astype(F32).astype(BF16)
-        )
-        back_ref[s : s + 1, :] = face
+
+    @pl.when(has_next)
+    def _():
+        pass_on(gotface_ref, prevface_ref, 4).start()
+
+    def face_tables(faces_ref, which):
+        for s in range(2 * N_SPAN):
+            face = faces_ref[s // 2][s % 2 : s % 2 + 1]
+            hot_ref[which, :, s * LANES : (s + 1) * LANES] = (
+                (lanes_high == (face & 127)).astype(F32).astype(BF16)
+            )
+            back_ref[which, s : s + 1, :] = face
+
+    face_tables(gotface_ref, 1)
 
     @pl.when(has_prev)
     def _():
-        await_bytes(prev_ref.at[0], recvs.at[1])
+        await_bytes(prev_ref, recvs.at[1])
 
     first_face = (c * N_NORMAL + n) * 1024
 
@@ -573,9 +602,15 @@
             total = total + weight_ref[k] * jnp.where(link >= 0, picked, 0.0)
         return total
 
-    run0 = runin(prev_ref[0], out_ref[0])
-
-    wait_normal(0, nr_ref)
+    run0 = runin(prev_ref[...], outflow0)
+    for i, value in enumerate((film0, shed, cool_ref[...], run0)):
+        pack_ref[i] = value
+
+    @pl.when(has_next)
+    def _():
+        pass_on(pack_ref, prevpack_ref, 2).start()
+
+    wait_normal(*first_halo)
 
     def edge_speed(side, present):
         @pl.when(present)
@@ -591,8 +626,24 @@
     edge_speed(0, has_low)
     edge_speed(1, has_high)
 
-    def first_layer(i):
-        x = layer_of(i)
+    again = span_copies(s1_ref, s1_ref, 2)
+
+    @pl.loop(0, NX)
+    def _(i):
+        @pl.when(i == 8)
+        def _():
+            start_normal(*again_halo[0])
+            for copy in spans:
+                copy.wait()
+            for edge in (0, NX + 1):
+                v0_ref[edge] = s_ref[1, edge] * (half_step / s_ref[0, edge])
+
+        @pl.when(i == 10)
+        def _():
+            for copy in again:
+                copy.start()
+
+        x = jnp.where(i < 8, i + 2, jnp.where(i == 8, 1, jnp.where(i == 9, NX, i)))
 
         def emit(t, zs, acc, v0, v1, v2):
             for k in range(4):
@@ -602,72 +653,67 @@
 
         advance(s_ref, v0_ref, v1_ref, v2_ref, vn_ref, nr_ref, air_ref, drag_ref, emit, x)
 
-    @pl.loop(0, FIRST_CUT)
-    def _(i):
-        first_layer(i)
+    start_normal(*again_halo[1])
+    start_normal(*again_halo[2])
+
+    @pl.when(has_prev)
+    def _():
+        await_bytes(prevface_ref, recvs.at[4])
+        await_bytes(prevpack_ref, recvs.at[2])
+
+    face_tables(prevface_ref, 0)
+
+    @pl.when(on_wall)
+    def _():
+        await_bytes(got_ref.at[pl.ds(0, N_SPAN - 1)], recvs.at[3])
 
     @pl.when(off_wall)
     def _():
-        await_bytes(part_ref, recvs.at[3])
-        to_row(part_ref, got_ref, 4)
-
-    got_ref[c] = part_ref[c]
-
-    @pl.loop(FIRST_CUT, NX)
-    def _(i):
-        @pl.when(i == NX - 2)
-        def _():
-            for copy in spans:
-                copy.wait()
-            for edge in (0, NX + 1):
-                v0_ref[edge] = s_ref[1, edge] * (half_step / s_ref[0, edge])
-
-        first_layer(i)
-
-    start_normal(1, nr2_ref)
-    again = span_copies(s1_ref, s1_ref, 2)
-    for copy in again:
-        copy.start()
-
-    await_bytes(got_ref.at[pl.ds(0, N_SPAN - 1)], recvs.at[4])
+        await_bytes(got_ref, recvs.at[3])
+
     eight = iota((8, LANES), 0)
-    for s in range(2 * N_SPAN):
-        at = eight == (back_ref[s : s + 1, :] >> 7)
-        values = [got_ref[s // 2][2 * v + s % 2 : 2 * v + s % 2 + 1] for v in range(2)]
-        highs = [value.astype(BF16).astype(F32) for value in values]
-        rows = []
-        for part in (highs, [values[v] - highs[v] for v in range(2)]):
-            rows.extend(jnp.where(at, part[v], 0.0) for v in range(2))
-        lhs_ref[:, s * LANES : (s + 1) * LANES] = jnp.concatenate(rows, axis=0).astype(BF16)
-    sums = lax.dot_general(lhs_ref[...], hot_ref[...], NT, preferred_element_type=F32)
-    sums = sums[:16] + sums[16:]
-    face_catch = sums[:8]
-    heat = cool_ref[...] / (1.0 + sums[8:])
-
-    def film_step(film, outflow, run):
-        inflow = impact_rate * face_catch + film - outflow + run
+
+    def face_sums(which):
+        for s in range(2 * N_SPAN):
+            at = eight == (back_ref[which, s : s + 1, :] >> 7)
+            values = [
+                got_ref[s // 2, which, 2 * v + s % 2 : 2 * v + s % 2 + 1, :] for v in range(2)
+            ]
+            highs = [value.astype(BF16).astype(F32) for value in values]
+            rows = []
+            for part in (highs, [values[v] - highs[v] for v in range(2)]):
+                rows.extend(jnp.where(at, part[v], 0.0) for v in range(2))
+            lhs_ref[which, :, s * LANES : (s + 1) * LANES] = (
+                jnp.concatenate(rows, axis=0).astype(BF16)
+            )
+        sums = lax.dot_general(
+            lhs_ref[which], hot_ref[which], NT, preferred_element_type=F32
+        )
+        sums = sums[:16] + sums[16:]
+        return sums[:8], sums[8:]
+
+    def film_step(film, outflow, run, catch, heat):
+        inflow = impact_rate * catch + film - outflow + run
         frozen = heat * inflow / (heat + inflow)
         return inflow - frozen, frozen
 
-    film1, frozen1 = film_step(film0, out_ref[0], run0)
-    out_ref[1] = film1 * shed
-
-    @pl.when(has_next)
-    def _():
-        pass_on(1).start()
-
-    @pl.when(has_prev)
-    def _():
-        await_bytes(prev_ref.at[1], recvs.at[2])
-
-    run1 = runin(prev_ref[1], out_ref[1])
-    film2, frozen2 = film_step(film1, out_ref[1], run1)
+    prev_catch, prev_kinetic = face_sums(0)
+    face_catch, face_kinetic = face_sums(1)
+    heat = cool_ref[...] / (1.0 + face_kinetic)
+    prev_film, prev_shed, prev_cool, prev_run = (prevpack_ref[i] for i in range(4))
+    prev_film1, _ = film_step(
+        prev_film, prev_ref[...], prev_run, prev_catch, prev_cool / (1.0 + prev_kinetic)
+    )
+    film1, frozen1 = film_step(film0, outflow0, run0, face_catch, heat)
+    outflow1 = film1 * shed
+    run1 = runin(prev_film1 * prev_shed, outflow1)
+    film2, frozen2 = film_step(film1, outflow1, run1, face_catch, heat)
     film_out[...] = film2
     ice2 = ice_ref[...] + frozen1 + frozen2
     ice_out[...] = ice2
 
     for g in range(4):
-        faces = back_ref[g * 8 : g * 8 + 8, :]
+        faces = back_ref[1, g * 8 : g * 8 + 8, :]
         low, high = faces & 127, faces >> 7
         picked = jnp.zeros((8, LANES), F32)
         for j in range(8):
@@ -678,20 +724,23 @@
             picked = jnp.where(high == j, value, picked)
         for i in range(4):
             col_ref[g * 4 + i] = picked[2 * i : 2 * i + 2]
-
-    @pl.loop(0, OWNERS - 1)
+    to_all(lambda there, side: col_ref.at[there], all_ref.at[c * N_NORMAL + n], 5)
+    all_ref[c * N_NORMAL + n] = col_ref[c]
+
+
+    @pl.loop(0, NX)
     def _(i):
-        there = row_peer(i >> 3)
-        side = 2 * far_first(n >> 1, (i >> 1) & 3) + ((n + 1 + i) & 1)
-        remote(col_ref.at[there], all_ref.at[n * N_SPAN + c], sends.at[5], recvs.at[5],
-               (there, side)).start()
-
-    all_ref[n * N_SPAN + c] = col_ref[c]
-
-    wait_normal(1, nr2_ref)
-
-    def second_layer(i):
-        x = layer_of(i)
+        for at, part in ((0, 0), (8, 1), (NX - 2, 2)):
+            @pl.when(i == at)
+            def _():
+                wait_normal(*again_halo[part])
+
+        @pl.when(i == NX - 2)
+        def _():
+            for copy in again:
+                copy.wait()
+
+        x = jnp.where(i < NX - 2, i + 2, jnp.where(i == NX - 2, 1, NX))
 
         def emit(t, zs, acc, v0, v1, v2):
             frac_out[x - 1, :, zs] = acc[0]
@@ -700,33 +749,21 @@
 
         advance(s1_ref, v0_ref, v1_ref, v2_ref, vn_ref, nr2_ref, air_ref, drag_ref, emit, x)
 
-    @pl.loop(0, NX)
-    def _(i):
-        @pl.when(i == NX - 2)
-        def _():
-            for copy in again:
-                copy.wait()
-
-        second_layer(i)
-
     await_bytes(all_ref.at[pl.ds(0, OWNERS - 1)], recvs.at[5])
 
     await_bytes(sendface_ref.at[pl.ds(0, N_SPAN - 1)], sends.at[0])
 
     @pl.when(has_next)
     def _():
-        await_bytes(out_ref.at[0], sends.at[1])
-        await_bytes(out_ref.at[1], sends.at[2])
+        await_bytes(out_ref, sends.at[1])
+        await_bytes(pack_ref, sends.at[2])
+        await_bytes(gotface_ref, sends.at[4])
 
     @pl.when(on_wall)
     def _():
-        await_bytes(fw_ref.at[pl.ds(0, OWNERS - N_SPAN)], sends.at[3])
-
-    await_bytes(part_ref.at[pl.ds(0, N_SPAN - 1)], sends.at[4])
+        await_bytes(gone_ref, sends.at[3])
+
     await_bytes(all_ref.at[pl.ds(0, OWNERS - 1)], sends.at[5])
-
-
-FIRST_CUT = 10
 
 
 def output_kernel(
@@ -758,13 +795,13 @@
         @pl.loop(g * group, (g + 1) * group)
         def _(x):
             key = key8_ref[x]
-            order, rank = key >> 5, key & (SLOTS - 1)
+            owner, rank = key >> 5, key & (SLOTS - 1)
             base = pl.multiple_of((x // 2) * SLOTS, SLOTS)
             table = pick_ref[pl.ds(base, SLOTS), :]
             picked = jnp.zeros((8, LANES), F32)
             for j in range(SLOTS):
                 value = jnp.take_along_axis(
-                    jnp.broadcast_to(table[j : j + 1], (8, LANES)), order, axis=1,
+                    jnp.broadcast_to(table[j : j + 1], (8, LANES)), owner, axis=1,
                     mode="promise_in_bounds",
                 )
                 picked = jnp.where(rank == j, value, picked)
@@ -837,20 +874,23 @@
             pltpu.VMEM((2, STRIP, 1, NZ), F32),
             pltpu.VMEM((2, STRIP, 1, NZ), F32),
             pltpu.VMEM((2, 8 * SLOTS, OWNERS), F32),
-            pltpu.VMEM((OWNERS, 4, LANES), F32),
-            pltpu.VMEM((N_SPAN, 4, LANES), F32),
-            pltpu.VMEM((N_SPAN, 4, LANES), F32),
+            pltpu.VMEM((OWNERS + 1, 4, LANES), F32),
+            pltpu.VMEM((N_SPAN, 2, 4, LANES), F32),
             pltpu.VMEM((N_SPAN, 2, LANES), I32),
-            pltpu.VMEM((32, 2 * N_SPAN * LANES), BF16),
-            pltpu.VMEM((LANES, 2 * N_SPAN * LANES), BF16),
+            pltpu.VMEM((N_SPAN, 2, LANES), I32),
+            pltpu.VMEM((2, 32, 2 * N_SPAN * LANES), BF16),
+            pltpu.VMEM((2, LANES, 2 * N_SPAN * LANES), BF16),
+            pltpu.VMEM((OWNERS - 1, 8, LANES), F32),
             pltpu.VMEM((4, 8, LANES), I32),
             pltpu.VMEM((4, 8, LANES), F32),
-            pltpu.VMEM((2, 8, LANES), F32),
-            pltpu.VMEM((2, 8, LANES), F32),
-            pltpu.VMEM((2 * N_SPAN, LANES), I32),
+            pltpu.VMEM((8, LANES), F32),
+            pltpu.VMEM((8, LANES), F32),
+            pltpu.VMEM((4, 8, LANES), F32),
+            pltpu.VMEM((4, 8, LANES), F32),
+            pltpu.VMEM((2, 2 * N_SPAN, LANES), I32),
             pltpu.VMEM((N_SPAN, 2, LANES), F32),
-            dma((10,)), dma((8,)), dma((4,)), dma((4,)), dma((4,)), dma((4,)), dma((2,)), dma((2,)),
-            dma((6,)), dma((6,)),
+            dma((10,)), dma((8,)), dma((4,)), dma((4,)), dma((8,)), dma((8,)), dma((2,)), dma((2,)),
+            dma((6,)), dma((6,)), pltpu.SemaphoreType.REGULAR,
         ],
         compiler_params=pltpu.CompilerParams(
             collective_id=0, has_side_effects=True, vmem_limit_bytes=40 * MB

time: 41.8 us -> 38.1 us (0.911)
  Pallas kernels: 40.8 us -> 37.3 us
    pallas_call x1, Pallas kernels: 38 us -> 34.6 us  [per_device(): pl.pallas_call(main_kernel, out_shape=(shape(brick), shape((3,) + brick),...]
where the time goes in v3:
time: 38.1 us; the launch traced here: 38 us
  Pallas kernels  37.3 us (98%)
  between operations  0.64 us (2%)
    pallas_call x1, Pallas kernels, per_device(): pl.pallas_call(main_kernel, out_shape=(shape(brick), shape((3,) + brick),...  34.6 us
    pallas_call x1, Pallas kernels, per_device(): pl.pallas_call(output_kernel, out_shape=(shape(brick), shape((3,) + brick...  2.78 us

profile of v3, /device:TPU:1, one launch (start us, length us, event | category | flops | bytes accessed | tf_op | source)
XLA Modules:
  0.0 38.0 jit_solution(13038334037016802579)
XLA Ops:
  0.6 34.6 %accretion.1 = (f32[16,16,1024]{2,1,0:T(8,128)S(1)}, f32[3,16,16,1024]{3,2,1,0:T(8,128)S(1)}, f32[8,128]{1,0:T(8,128)S(1)}, f32[8,128]{1,0:T(8,128)S(1)}, f32[12...) custom-call(f32[16,16,1024]{2,1,0:T(8,128)} %a_hbm.1, f32[3,16,16,1024]{3,2,1,0:T(8,128)} %m_hbm.1, ...), custom_call_target="tpu_custom_call" | custom-call | tf_op jit(solution)/shard_map/accretion/pallas_call | solution.py:839
  35.2 2.8 %results.1 = (f32[16,16,1024]{2,1,0:T(8,128)}, f32[3,16,16,1024]{3,2,1,0:T(8,128)}, f32[8,128]{1,0:T(8,128)}, f32[8,128]{1,0:T(8,128)}, f32[16,16,1024]{2,1,0:T(8,128)}) custom-call(f32[16,16,1024]{2,1,0:T(8,128)S(1)} %get-tuple-element.16.frac_ref, f32[3,16,16,1024]{3,2,1,0:T(8,128)S(1)} %get-tuple-element.17.mom_ref, ...), custom_call_target="tpu_custom_call" | custom-call | tf_op jit(solution)/shard_map/results/pallas_call | solution.py:911

commit v4 on v3

--- a/solution.py
+++ b/solution.py
@@ -476,11 +476,11 @@
             ns_ref[0, 0, k, x] = s_ref[k, x + 1, 0:1, :]
             ns_ref[0, 1, k, x] = s_ref[k, x + 1, NYB - 1 : NYB, :]
 
-    first_halo = (0, nr_ref, 0, 0, NX)
-    again_halo = [
-        (1, nr2_ref, 1 + i, start, size) for i, (start, size) in enumerate(((1, 8), (9, 7), (0, 1)))
-    ]
-    start_normal(*first_halo)
+    parts = ((1, 8), (9, 7), (0, 1))
+    first_halo = [(0, nr_ref, i, start, size) for i, (start, size) in enumerate(parts)]
+    again_halo = [(1, nr2_ref, 3 + i, start, size) for i, (start, size) in enumerate(parts)]
+    for halo in first_halo:
+        start_normal(*halo)
     close_edges(nr_ref)
     close_edges(nr2_ref)
     spans = span_copies(s_ref, s_ref, 0)
@@ -563,12 +563,8 @@
         for t in range(8):
             links_ref[k, t : t + 1, :] = up_ref[k : k + 1, t * LANES : (t + 1) * LANES]
             weight_ref[k, t : t + 1, :] = share_ref[k : k + 1, t * LANES : (t + 1) * LANES]
-    await_bytes(gotface_ref.at[pl.ds(0, N_SPAN - 1)], recvs.at[0])
     lanes_high = iota((LANES, LANES), 0)
-
-    @pl.when(has_next)
-    def _():
-        pass_on(gotface_ref, prevface_ref, 4).start()
+    first_face = (c * N_NORMAL + n) * 1024
 
     def face_tables(faces_ref, which):
         for s in range(2 * N_SPAN):
@@ -577,14 +573,6 @@
                 (lanes_high == (face & 127)).astype(F32).astype(BF16)
             )
             back_ref[which, s : s + 1, :] = face
-
-    face_tables(gotface_ref, 1)
-
-    @pl.when(has_prev)
-    def _():
-        await_bytes(prev_ref, recvs.at[1])
-
-    first_face = (c * N_NORMAL + n) * 1024
 
     def runin(before, own):
         total = jnp.zeros((8, LANES), F32)
@@ -602,30 +590,45 @@
             total = total + weight_ref[k] * jnp.where(link >= 0, picked, 0.0)
         return total
 
-    run0 = runin(prev_ref[...], outflow0)
-    for i, value in enumerate((film0, shed, cool_ref[...], run0)):
-        pack_ref[i] = value
-
-    @pl.when(has_next)
-    def _():
-        pass_on(pack_ref, prevpack_ref, 2).start()
-
-    wait_normal(*first_halo)
-
-    def edge_speed(side, present):
+    def link_up():
+        await_bytes(gotface_ref.at[pl.ds(0, N_SPAN - 1)], recvs.at[0])
+
+        @pl.when(has_next)
+        def _():
+            pass_on(gotface_ref, prevface_ref, 4).start()
+
+        face_tables(gotface_ref, 1)
+
+        @pl.when(has_prev)
+        def _():
+            await_bytes(prev_ref, recvs.at[1])
+
+        run0 = runin(prev_ref[...], outflow0)
+        for i, value in enumerate((film0, shed, cool_ref[...], run0)):
+            pack_ref[i] = value
+
+        @pl.when(has_next)
+        def _():
+            pass_on(pack_ref, prevpack_ref, 2).start()
+
+    def edge_speed(side, present, start, size):
         @pl.when(present)
         def _():
-            @pl.loop(0, NX)
+            @pl.loop(start, start + size)
             def _(x):
                 vn_ref[side, x] = nr_ref[side, 2, x] * (half_step / nr_ref[side, 0, x])
 
+    for side, present in ((0, has_low), (1, has_high)):
         @pl.when(jnp.logical_not(present))
         def _():
             vn_ref[side] = jnp.zeros(vn_ref.shape[1:], F32)
 
-    edge_speed(0, has_low)
-    edge_speed(1, has_high)
-
+    def take_halo(part):
+        wait_normal(*first_halo[part])
+        for side, present in ((0, has_low), (1, has_high)):
+            edge_speed(side, present, *parts[part])
+
+    take_halo(0)
     again = span_copies(s1_ref, s1_ref, 2)
 
     @pl.loop(0, NX)
@@ -633,6 +636,9 @@
         @pl.when(i == 8)
         def _():
             start_normal(*again_halo[0])
+            link_up()
+            take_halo(1)
+            take_halo(2)
             for copy in spans:
                 copy.wait()
             for edge in (0, NX + 1):
@@ -699,6 +705,7 @@
 
     prev_catch, prev_kinetic = face_sums(0)
     face_catch, face_kinetic = face_sums(1)
+    run0 = pack_ref[3]
     heat = cool_ref[...] / (1.0 + face_kinetic)
     prev_film, prev_shed, prev_cool, prev_run = (prevpack_ref[i] for i in range(4))
     prev_film1, _ = film_step(
@@ -889,7 +896,7 @@
             pltpu.VMEM((4, 8, LANES), F32),
             pltpu.VMEM((2, 2 * N_SPAN, LANES), I32),
             pltpu.VMEM((N_SPAN, 2, LANES), F32),
-            dma((10,)), dma((8,)), dma((4,)), dma((4,)), dma((8,)), dma((8,)), dma((2,)), dma((2,)),
+            dma((10,)), dma((8,)), dma((4,)), dma((4,)), dma((12,)), dma((12,)), dma((2,)), dma((2,)),
             dma((6,)), dma((6,)), pltpu.SemaphoreType.REGULAR,
         ],
         compiler_params=pltpu.CompilerParams(

time: 38.1 us -> 37.9 us (level)
  the two profiles are of different devices: /device:TPU:1 before, /device:TPU:0 now
where the time goes in v4:
time: 37.9 us; the launch traced here: 37.8 us
  Pallas kernels  37.2 us (98%)
  between operations  0.64 us (2%)
    pallas_call x1, Pallas kernels, per_device(): pl.pallas_call(main_kernel, out_shape=(shape(brick), shape((3,) + brick),...  34.4 us
    pallas_call x1, Pallas kernels, per_device(): pl.pallas_call(output_kernel, out_shape=(shape(brick), shape((3,) + brick...  2.78 us

profile of v4, /device:TPU:0, one launch (start us, length us, event | category | flops | bytes accessed | tf_op | source)
XLA Modules:
  0.0 37.8 jit_solution(14991566541431630666)
XLA Ops:
  0.6 34.4 %accretion.1 = (f32[16,16,1024]{2,1,0:T(8,128)S(1)}, f32[3,16,16,1024]{3,2,1,0:T(8,128)S(1)}, f32[8,128]{1,0:T(8,128)S(1)}, f32[8,128]{1,0:T(8,128)S(1)}, f32[12...) custom-call(f32[16,16,1024]{2,1,0:T(8,128)} %a_hbm.1, f32[3,16,16,1024]{3,2,1,0:T(8,128)} %m_hbm.1, ...), custom_call_target="tpu_custom_call" | custom-call | tf_op jit(solution)/shard_map/accretion/pallas_call | solution.py:846
  35.0 2.8 %results.1 = (f32[16,16,1024]{2,1,0:T(8,128)}, f32[3,16,16,1024]{3,2,1,0:T(8,128)}, f32[8,128]{1,0:T(8,128)}, f32[8,128]{1,0:T(8,128)}, f32[16,16,1024]{2,1,0:T(8,128)}) custom-call(f32[16,16,1024]{2,1,0:T(8,128)S(1)} %get-tuple-element.16.frac_ref, f32[3,16,16,1024]{3,2,1,0:T(8,128)S(1)} %get-tuple-element.17.mom_ref, ...), custom_call_target="tpu_custom_call" | custom-call | tf_op jit(solution)/shard_map/results/pallas_call | solution.py:918
